TPU v7x, 32 devices: a whole 2x2x4 slice. The times are simulated.
32 devices in a mesh: rep: 2 (over y), seq: 4 (over z), mp: 2 (over x), sub: 2 (over core).
Axes of the slice: x: 2, y: 2, z: 4, core: 2. Of those that a mesh axis runs over, the one named last changes fastest.
Arguments:
- normed_inputs: bfloat16 [4096, 5120], P(('rep', 'seq', 'sub'), 'mp'), parts along dimension 0, may hold values from -6 to 6
- base_queries: bfloat16 [4096, 8192], P(('rep', 'seq', 'sub'), 'mp'), parts along dimension 0, may hold values from -8 to 8
- base_keys: bfloat16 [4096, 1024], P(('rep', 'seq', 'sub'), 'mp'), parts along dimension 0, may hold values from -8 to 8
- base_values: bfloat16 [4096, 1024], P(('rep', 'seq', 'sub'), 'mp'), parts along dimension 0, may hold values from -6 to 6
- adapter_down: bfloat16 [8, 5120, 16], P(None, 'mp'), may hold values from -0.078125 to 0.078125
- adapter_up: bfloat16 [8, 16, 8192], P(None, None, 'mp'), may hold values from -0.75 to 0.75
- position_document: int32 [4096], P(('rep', 'seq', 'sub')), parts along dimension 0, may hold values from 0 to 15, never falling along the last dimension, each value on 1 to 768 neighbouring positions
- document_tenant: int32 [32], P('rep'), parts along dimension 0, may hold values from 0 to 7, as said below
- output_gradient: bfloat16 [4096, 8192], P(('rep', 'seq', 'sub'), 'mp'), parts along dimension 0, may hold values from -6 to 6
Outputs:
- attn_out: bfloat16 [4096, 8192], P(('rep', 'seq', 'sub'), 'mp'), parts along dimension 0
- grad_a: float32 [16, 5120, 16], P('rep', 'mp'), parts along dimension 0
- grad_b: float32 [16, 16, 8192], P('rep', None, 'mp'), parts along dimension 0
There are 2 independent parts, one for each index of `rep`. A program takes and returns all parts, laid end to end along the dimension named above; an argument that names none is the same for every part. Nothing has to cross between parts.
Inputs may be any that keep to these rules, and one draw needn't show every extreme that they name: `position_document`: Non-decreasing along the row; each document spans 1 to 768 positions, and one spans exactly that many. `document_tenant`: every tenant owns exactly 2 documents.
All inputs are finite; a program needn't handle non-finite values.
Results may differ from a plain program's by a relative error of at most 0.035.
Values may be sent and summed in bfloat16 or wider, within the bound.
No kernel may reach another device: no remote copies, remote signals or barrier semaphores. Data moves between devices by JAX's collectives and lax.ppermute only.
A program may use at most 192 MiB of HBM per device.

v0:
```python
import functools

import jax
import jax.numpy as jnp
from jax import lax
from jax.experimental import pallas as pl
from jax.experimental.pallas import tpu as pltpu
from jax.sharding import PartitionSpec as P

HEAD = 128
REACH = 3
NEG = -1e30
LIFT = 2.0
LOG2E = 1.4426950408889634
TAIL = 16
VMEM_BYTES = 48 * 1024 * 1024
VMEM_MOST = 60 * 1024 * 1024
VMEM_HEADS = 57 * 1024 * 1024

VM = pl.BlockSpec(memory_space=pltpu.VMEM)
SM = pl.BlockSpec(memory_space=pltpu.SMEM)
ANY = pl.BlockSpec(memory_space=pl.ANY)


def nt(a, b):
    return lax.dot_general(a, b, (((1,), (1,)), ((), ())), preferred_element_type=jnp.float32)


def nn(a, b):
    return jnp.dot(a, b, preferred_element_type=jnp.float32)


def params(limit=VMEM_BYTES):
    return pltpu.CompilerParams(vmem_limit_bytes=limit)


def fetch(pairs, sems):
    copies = [pltpu.make_async_copy(src, dst, sems.at[i]) for i, (src, dst) in enumerate(pairs)]
    for copy in copies:
        copy.start()
    return copies


def pack_kernel(counts, keys, values, doc, *rest):
    outs, (ids, blocks, tail, sems) = rest[: len(counts)], rest[len(counts) :]
    rows, width = keys.shape
    loads = fetch(
        [(doc, ids), (keys, blocks.at[0]), (values, blocks.at[1])], sems.at[pl.ds(0, 3)]
    )
    loads[0].wait()
    tail[...] = jnp.zeros_like(tail)
    tail[:, 0:rows] = jnp.broadcast_to((ids[...] + 1).astype(jnp.float32), (TAIL, rows)).astype(
        jnp.bfloat16
    )
    pairs, first = [(tail, outs[0].at[pl.ds(rows, TAIL), :])], 0
    for count, out in zip(counts, outs):
        for half in range(2):
            source = blocks.at[half, :, pl.ds(first * HEAD, count * HEAD)]
            pairs.append((source, out.at[pl.ds(0, rows), pl.ds(half * count * HEAD, count * HEAD)]))
        first += count
    loads[1].wait()
    loads[2].wait()
    for copy in fetch(pairs, sems.at[pl.ds(3, len(pairs))]):
        copy.wait()


def pack(keys, values, doc, counts):
    rows, width = keys.shape
    shapes = [
        jax.ShapeDtypeStruct((rows + (0 if i else TAIL), 2 * count * HEAD), jnp.bfloat16)
        for i, count in enumerate(counts)
    ]
    return pl.pallas_call(
        functools.partial(pack_kernel, counts),
        out_shape=shapes,
        in_specs=[ANY] * 3,
        out_specs=[ANY] * len(counts),
        scratch_shapes=[
            pltpu.VMEM((1, rows), jnp.int32),
            pltpu.VMEM((2, rows, width), jnp.bfloat16),
            pltpu.VMEM((TAIL, shapes[0].shape[1]), jnp.bfloat16),
            pltpu.SemaphoreType.DMA((4 + 2 * len(counts),)),
        ],
        compiler_params=params(VMEM_MOST),
        cost_estimate=pl.CostEstimate(flops=0, bytes_accessed=8 * rows * width, transcendentals=0),
        name="pack_keys_values",
    )(keys, values, doc)


def relay_kernel(own, got, after, out, held, sems):
    sub = lax.axis_index("sub")

    def move(source):
        load = pltpu.make_async_copy(source, held, sems.at[0])
        load.start()
        load.wait()

    @pl.when(sub == 0)
    def _():
        move(own)

    @pl.when(sub != 0)
    def _():
        move(got)

    store = pltpu.make_async_copy(held, out, sems.at[1])
    store.start()
    store.wait()


def relay(own, got, after):
    return pl.pallas_call(
        relay_kernel,
        out_shape=jax.ShapeDtypeStruct(own.shape, own.dtype),
        in_specs=[ANY, ANY, ANY],
        out_specs=ANY,
        scratch_shapes=[pltpu.VMEM(own.shape, own.dtype), pltpu.SemaphoreType.DMA((2,))],
        compiler_params=params(),
        cost_estimate=pl.CostEstimate(flops=0, bytes_accessed=4 * own.size, transcendentals=0),
        name="relay_block",
    )(own, got, after)


def selector_of(owner, tenants, rank):
    rows = owner.shape[1]
    tenant = lax.broadcasted_iota(jnp.int32, (tenants * rank, rows), 0) // rank
    return tenant == owner


def fold(full, owner, tenants, rank):
    kept = jnp.where(selector_of(owner, tenants, rank), full, 0.0)
    total = kept[0:rank]
    for t in range(1, tenants):
        total = total + kept[t * rank : (t + 1) * rank]
    return total


def unfold(compact, owner, tenants, rank):
    spread = jnp.concatenate([compact] * tenants, axis=0)
    return jnp.where(selector_of(owner, tenants, rank), spread, 0.0)


def down_kernel(tenants, rank, x_hbm, adapter_hbm, doc_hbm, tenant_of, info, x, adapter, doc, sems):
    copies = fetch([(doc_hbm, doc), (x_hbm, x), (adapter_hbm, adapter)], sems)
    copies[0].wait()
    ids = doc[...]
    found = jnp.zeros(ids.shape, jnp.int32)
    for s in range(tenant_of.shape[0]):
        found = jnp.where(ids == s, tenant_of[s], found)
    info[rank:, :] = jnp.broadcast_to(found.astype(jnp.float32), (info.shape[0] - rank, ids.shape[1]))
    copies[1].wait()
    copies[2].wait()
    info[0:rank, :] = fold(nt(x[...], adapter[...]).T, found, tenants, rank)


def down_project(x, adapter, doc, tenant_of, tenants, rank):
    rows, width = x.shape
    return pl.pallas_call(
        functools.partial(down_kernel, tenants, rank),
        out_shape=jax.ShapeDtypeStruct((rank + 8, rows), jnp.float32),
        in_specs=[ANY, ANY, ANY, SM],
        out_specs=VM,
        scratch_shapes=[
            pltpu.VMEM(x.shape, x.dtype),
            pltpu.VMEM(adapter.shape, adapter.dtype),
            pltpu.VMEM(doc.shape, doc.dtype),
            pltpu.SemaphoreType.DMA((3,)),
        ],
        compiler_params=params(VMEM_MOST),
        cost_estimate=pl.CostEstimate(
            flops=2 * rows * width * tenants * rank,
            bytes_accessed=2 * width * (rows + tenants * rank),
            transcendentals=0,
        ),
        name="down_project",
    )(x, adapter, doc, tenant_of)


def owner_of(info, rank):
    return info[rank : rank + 1, :].astype(jnp.int32)


def attention(chunk, chunks, base, grad, up, blocks, first, info, terms, before, tenants, rank):
    rows, width = base.shape
    count = blocks[0].shape[1] // (2 * HEAD)
    window = (REACH + 1) * rows
    tall = tenants * rank
    half = tall // 2
    group = width // HEAD // (count * chunks)
    span = group * HEAD
    pair = min(4, group)
    scale = HEAD**-0.5
    offset = chunk * count
    wide = lambda r: pl.BlockSpec((r, span), lambda i: (0, i + offset))
    narrow = pl.BlockSpec((half, span), lambda i: (0, i))
    keys = pl.BlockSpec((rows, HEAD), lambda i: (0, i))
    values = pl.BlockSpec((rows, HEAD), lambda i: (0, i + count))
    ids = pl.BlockSpec((TAIL, rows), lambda i: (rows // TAIL, 0))
    same = lambda a: pl.BlockSpec(a.shape, lambda i: (0, 0))
    operands, specs = [base, grad, up], [wide(rows), wide(rows), wide(tall)]
    for block in blocks:
        operands += [block, block]
        specs += [keys, values]
    operands += [*first, info, *terms]
    specs += [ids] * 4 + [same(info)] * 3
    if before is not None:
        operands += [before[1], before[0]]
        specs += [same(before[1]), ANY]
    held = dict(
        kw=pltpu.VMEM((window, HEAD), jnp.bfloat16),
        vw=pltpu.VMEM((window, HEAD), jnp.bfloat16),
        kt=pltpu.VMEM((HEAD, window), jnp.bfloat16),
        vt=pltpu.VMEM((HEAD + TAIL, window), jnp.bfloat16),
        bottle=pltpu.VMEM((rows, tall), jnp.bfloat16),
        bottle_t=pltpu.VMEM((tall, rows), jnp.bfloat16),
        bias=pltpu.VMEM((window, rows), jnp.float32),
        query=pltpu.VMEM((rows, span), jnp.bfloat16),
        gquery=pltpu.VMEM((span, rows), jnp.bfloat16),
        scores=pltpu.VMEM((pair, window, rows), jnp.float32),
        part=pltpu.VMEM((tall, span), jnp.bfloat16),
        total=pltpu.VMEM((tall, rows), jnp.float32),
        reach=pltpu.SMEM((1,), jnp.int32),
    )

    def kernel(*refs):
        base, grad, up = refs[0:3]
        kv, tails, info, terms = refs[3:11], refs[11:15], refs[15], refs[16:18]
        out, keep, send, projected = refs[len(operands) : len(operands) + 4]
        r = dict(zip(held, refs[len(operands) + 4 :]))
        kw, vw, kt, vt = (r[n] for n in ("kw", "vw", "kt", "vt"))
        bias, query, gquery, scores = (r[n] for n in ("bias", "query", "gquery", "scores"))
        sub = lax.axis_index("sub")
        step = pl.program_id(0)

        @pl.when(step == 0)
        def _():
            owner = owner_of(info, rank)
            lifted = unfold((terms[0][...] + terms[1][...])[0:rank], owner, tenants, rank)
            r["bottle_t"][...] = lifted.astype(jnp.bfloat16)
            r["bottle"][...] = lifted.T.astype(jnp.bfloat16)
            r["total"][...] = jnp.zeros((tall, rows), jnp.float32)
            vt[HEAD:, :] = jnp.ones((TAIL, window), jnp.bfloat16)
            own, two, swap, passed = (ref[...].astype(jnp.float32) for ref in tails)
            near = jnp.where(sub == 0, swap, passed)
            far = jnp.where(sub == 0, passed, swap)
            mine = own[0:1, :]
            lowest = jnp.min(mine)
            reach = 0
            for slot, block in ((REACH, own), (2, near), (1, two), (0, far)):
                same = block.T[:, 0:1] == mine
                if slot == REACH:
                    same = same & (
                        lax.broadcasted_iota(jnp.int32, (rows, rows), 0)
                        <= lax.broadcasted_iota(jnp.int32, (rows, rows), 1)
                    )
                else:
                    reach = jnp.where(jnp.max(block[0:1, :]) == lowest, REACH - slot, reach)
                bias[slot * rows : (slot + 1) * rows, :] = jnp.where(same, 0.0, NEG)
            r["reach"][0] = reach

        def place(slot, k_ref, v_ref):
            at = slice(slot * rows, (slot + 1) * rows)
            k, v = k_ref[...], v_ref[...]
            kw[at, :] = k
            vw[at, :] = v
            kt[:, at] = k.T
            vt[0:HEAD, at] = v.T

        place(REACH, *kv[0:2])
        place(1, *kv[2:4])

        @pl.when(sub == 0)
        def _():
            place(2, *kv[4:6])
            place(0, *kv[6:8])

        @pl.when(sub != 0)
        def _():
            place(2, *kv[6:8])
            place(0, *kv[4:6])

        query[...] = (
            base[...].astype(jnp.float32) + LIFT * nn(r["bottle"][...], up[...])
        ).astype(jnp.bfloat16)
        ones = jnp.ones((TAIL, 2 * HEAD), jnp.bfloat16)

        def run(reached, numbers):
            chunks = [slice(c * rows, (c + 1) * rows) for c in range(REACH - reached, REACH + 1)]
            spans = [pl.ds(pl.multiple_of(h * HEAD, HEAD), HEAD) for h in numbers]
            peaks = []
            for i, span_i in enumerate(spans):
                q, peak = query[:, span_i], None
                for c in chunks:
                    s = nt(kw[c, :], q) + bias[c, :]
                    scores[i, c, :] = s
                    top = jnp.max(s, axis=0, keepdims=True)
                    peak = top if peak is None else jnp.maximum(peak, top)
                peaks.append(peak)
            inverses, rowdots = [], []
            for i, span_i in enumerate(spans):
                total = None
                for c in chunks:
                    w = jnp.exp2((scores[i, c, :] - peaks[i]) * (scale * LOG2E))
                    scores[i, c, :] = w
                    o = nn(vt[:, c], w.astype(jnp.bfloat16))
                    total = o if total is None else total + o
                inverse = 1.0 / total[HEAD : HEAD + 1, :]
                attn = (total[0:HEAD, :] * inverse).astype(jnp.bfloat16).T
                out[:, span_i] = attn
                product = grad[:, span_i].astype(jnp.float32) * attn.astype(jnp.float32)
                high = product.astype(jnp.bfloat16)
                low = (product - high.astype(jnp.float32)).astype(jnp.bfloat16)
                rowdots.append(nt(ones, jnp.concatenate([high, low], axis=1))[0:1, :])
                inverses.append(inverse)
            for i, span_i in enumerate(spans):
                g, moved = grad[:, span_i], None
                for c in chunks:
                    dprob = nt(vw[c, :], g)
                    ds = (scores[i, c, :] * (dprob - rowdots[i])).astype(jnp.bfloat16)
                    dq = nn(kt[:, c], ds)
                    moved = dq if moved is None else moved + dq
                gquery[span_i, :] = (moved * (inverses[i] * (LIFT * scale))).astype(jnp.bfloat16)

        for reached in range(REACH + 1):

            @pl.when(r["reach"][0] == reached)
            def _():
                @pl.loop(0, group // pair)
                def _(i):
                    run(reached, [i * pair + k for k in range(pair)])

        r["part"][...] = nt(r["bottle_t"][...], gquery[...]).astype(jnp.bfloat16)
        keep[...] = r["part"][pl.ds(pl.multiple_of(sub * half, half), half), :]
        send[...] = r["part"][pl.ds(pl.multiple_of((1 - sub) * half, half), half), :]
        r["total"][...] += nn(up[...], gquery[...])

        @pl.when(step == count - 1)
        def _():
            folded = fold(r["total"][...], owner_of(info, rank), tenants, rank)
            projected[...] = folded if before is None else folded + refs[18][...]

    return pl.pallas_call(
        kernel,
        grid=(count,),
        out_shape=[
            jax.ShapeDtypeStruct((rows, width), jnp.bfloat16),
            *halves_of(tall, count * span),
            jax.ShapeDtypeStruct((rank, rows), jnp.float32),
        ],
        in_specs=specs,
        out_specs=[wide(rows), narrow, narrow, pl.BlockSpec((rank, rows), lambda i: (0, 0))],
        scratch_shapes=list(held.values()),
        input_output_aliases={19: 0} if before is not None else {},
        compiler_params=params(VMEM_HEADS),
        cost_estimate=pl.CostEstimate(
            flops=8 * rows * window * span * count,
            bytes_accessed=6 * rows * span * count,
            transcendentals=rows * window * group * count,
        ),
        name="attention",
    )(*operands)


def small_call(kernel, name, shapes, *operands, after=(), through=(), scratch=()):
    size = sum(2 * a.size for a in operands)
    count, results = len(operands), jax.tree.leaves(shapes)
    given = (*operands, *after, *through)
    outs = len(given) + len(results)
    calls = pl.pallas_call(
        lambda *refs: kernel(
            *refs[:count], *refs[len(given) : outs], *refs[outs + len(through) :]
        ),
        out_shape=results + [jax.ShapeDtypeStruct(a.shape, a.dtype) for a in through],
        in_specs=[VM] * count + [ANY] * (len(after) + len(through)),
        out_specs=[VM] * len(results) + [ANY] * len(through),
        scratch_shapes=list(scratch),
        input_output_aliases={
            count + len(after) + i: len(results) + i for i in range(len(through))
        },
        compiler_params=params(),
        cost_estimate=pl.CostEstimate(flops=size, bytes_accessed=2 * size, transcendentals=0),
        name=name,
    )(*given)
    return calls if isinstance(shapes, list) or through else calls[0]


def grad_a_of(tenants, rank, one, other, info, x):
    g = unfold((one[...] + other[...]), owner_of(info[...], rank), tenants, rank)
    return nn(g.astype(jnp.bfloat16), x[...]).astype(jnp.bfloat16)


def grad_a_kernel(tenants, rank, one, other, info, x, out):
    out[...] = grad_a_of(tenants, rank, one, other, info, x)


def split_kernel(tenants, rank, one, other, info, x, keep, send):
    part = grad_a_of(tenants, rank, one, other, info, x)
    half = keep.shape[0]
    sub = lax.axis_index("sub")

    @pl.when(sub == 0)
    def _():
        keep[...] = part[0:half, :]
        send[...] = part[half:, :]

    @pl.when(sub != 0)
    def _():
        keep[...] = part[half:, :]
        send[...] = part[0:half, :]


def scatter_kernel(size, count, *refs):
    mine, *sends, total = refs[2 * count :]
    col = 0
    for keep, got in zip(refs[0 : 2 * count : 2], refs[1 : 2 * count : 2]):
        both = keep[...].astype(jnp.float32) + got[...].astype(jnp.float32)
        total[:, col : col + keep.shape[1]] = both.astype(jnp.bfloat16)
        col += keep.shape[1]
    me = lax.axis_index("seq")
    rows = mine.shape[0]
    for d, out in enumerate((mine, *sends)):
        at = pl.multiple_of(lax.rem(me + d, size) * rows, rows)
        out[...] = total[pl.ds(at, rows), :]


def sum_kernel(*refs):
    total = refs[0][...].astype(jnp.float32)
    for ref in refs[1:-1]:
        total = total + ref[...].astype(jnp.float32)
    refs[-1][...] = total.astype(jnp.bfloat16)


def gather_kernel(size, *refs):
    pieces, out = refs[:-1], refs[-1]
    me = lax.axis_index("seq")
    rows = pieces[0].shape[0]
    for d, piece in enumerate(pieces):
        at = pl.multiple_of(lax.rem(me + size - d, size) * rows, rows)
        out[pl.ds(at, rows), :] = piece[...]


def gather(pieces, after=()):
    size, (rows, width) = len(pieces), pieces[0].shape
    return small_call(
        functools.partial(gather_kernel, size), "gather_grads",
        jax.ShapeDtypeStruct((rows * size, width), jnp.bfloat16), *pieces, after=after,
    )


def finish_kernel(half_ref, other_ref, out):
    sub = lax.axis_index("sub")
    half = half_ref.shape[0]
    here = pl.ds(pl.multiple_of(sub * half, half), half)
    there = pl.ds(pl.multiple_of((1 - sub) * half, half), half)
    out[here, :] = half_ref[...].astype(jnp.float32)
    out[there, :] = other_ref[...].astype(jnp.float32)


def finish(half, other):
    rows, width = half.shape
    return small_call(
        finish_kernel, "finish_grads", jax.ShapeDtypeStruct((2 * rows, width), jnp.float32),
        half, other,
    )


def halves_of(rows, width):
    return [jax.ShapeDtypeStruct((rows // 2, width), jnp.bfloat16)] * 2


def scatter(*pairs, after=()):
    size = lax.axis_size("seq")
    rows, width = pairs[0][0].shape[0], sum(keep.shape[1] for keep, _ in pairs)
    shard = jax.ShapeDtypeStruct((rows // size, width), jnp.bfloat16)
    return small_call(
        functools.partial(scatter_kernel, size, len(pairs)), "scatter_grads", [shard] * size,
        *[block for pair in pairs for block in pair],
        after=after, scratch=[pltpu.VMEM((rows, width), jnp.bfloat16)],
    )


def exchange(shards):
    return [shards[0]] + [rotate_over(block, "seq", d + 1) for d, block in enumerate(shards[1:])]


def add_up(pieces, after=(), through=()):
    shape = jax.ShapeDtypeStruct(pieces[0].shape, pieces[0].dtype)
    return small_call(sum_kernel, "sum_grads", shape, *pieces, after=after, through=through)


def spread(shard):
    return [shard] + [rotate_over(shard, "seq", d) for d in range(1, lax.axis_size("seq"))]


def swap_over(block, axis):
    return lax.ppermute(block, axis, [(0, 1), (1, 0)])


def rotate_over(block, axis, d):
    size = lax.axis_size(axis)
    return lax.ppermute(block, axis, [(i, (i + d) % size) for i in range(size)])


def terms_over(block, axis):
    if lax.axis_size(axis) == 2:
        return block, swap_over(block, axis)
    return lax.psum(block, axis), jnp.zeros_like(block)


def shift_over(block, axis):
    size = lax.axis_size(axis)
    return lax.ppermute(block, axis, [(i, i + 1) for i in range(size - 1)])


def body(
    normed_inputs, base_queries, base_keys, base_values, adapter_down, adapter_up,
    position_document, document_tenant, output_gradient,
):
    rows, width = normed_inputs.shape
    tenants, _, rank = adapter_down.shape
    tall, up_width = tenants * rank, adapter_up.shape[2]
    doc = position_document.reshape(1, rows)
    adapter = jnp.transpose(adapter_down, (0, 2, 1)).reshape(tall, width)
    up = adapter_up.reshape(tall, up_width)
    key_heads = base_keys.shape[1] // HEAD
    chunks = 2 if key_heads % 2 == 0 else 1
    counts = (key_heads // chunks,) * chunks
    size = lax.axis_size("seq")
    by_hand = tall % (2 * TAIL * size) == 0

    own = pack(base_keys, base_values, doc, counts)
    two = [shift_over(block, "seq") for block in own]
    info = down_project(normed_inputs, adapter, doc, document_tenant, tenants, rank)
    swapped = [swap_over(block, "sub") for block in two]
    passed = [shift_over(relay(o, t, info), ("seq", "sub")) for o, t in zip(own, two)]
    terms = terms_over(info, "mp")
    first = (own[0], two[0], swapped[0], passed[0])

    state, pairs = None, []
    for c in range(chunks):
        out, keep, send, gdown = attention(
            c, chunks, base_queries, output_gradient, up,
            (own[c], two[c], swapped[c], passed[c]), first, info, terms, state, tenants, rank,
        )
        state = (out, gdown)
        pairs.append((keep, send))
    one, other = terms_over(gdown, "mp")
    if by_hand:
        shards_b = scatter(*[(keep, swap_over(send, "sub")) for keep, send in pairs])
        keep, send = small_call(
            functools.partial(split_kernel, tenants, rank), "split_grads", halves_of(tall, width),
            one, other, info, normed_inputs, after=shards_b[:1],
        )
        pieces_b = exchange(shards_b)
        shards_a = scatter((keep, swap_over(send, "sub")))
        pieces_a = exchange(shards_a)
        all_b = spread(add_up(pieces_b, after=shards_a[:1]))
        sum_a = add_up(pieces_a)
        half_b = gather(all_b, after=[sum_a])
        other_b = swap_over(half_b, "sub")
        half_a = gather(spread(sum_a), after=[other_b])
        grad_b = finish(half_b, other_b)
        grad_a = finish(half_a, swap_over(half_a, "sub"))
    else:
        part_a = small_call(
            functools.partial(grad_a_kernel, tenants, rank), "grad_a_part",
            jax.ShapeDtypeStruct((tall, width), jnp.bfloat16), one, other, info, normed_inputs,
        )
        grad_a = lax.psum(part_a, ("seq", "sub")).astype(jnp.float32)
        keeps = jnp.concatenate([keep for keep, _ in pairs], axis=1)
        sends = jnp.concatenate([send for _, send in pairs], axis=1)
        low = lax.axis_index("sub") == 0
        part_b = jnp.concatenate([jnp.where(low, keeps, sends), jnp.where(low, sends, keeps)])
        grad_b = lax.psum(part_b, ("seq", "sub")).astype(jnp.float32)
    grad_a = jnp.transpose(grad_a.reshape(tenants, rank, width), (0, 2, 1))
    return out, grad_a, grad_b.reshape(tenants, rank, up_width)


def solution(mesh):
    split = P(("rep", "seq", "sub"), "mp")
    in_specs = (
        split, split, split, split, P(None, "mp", None), P(None, None, "mp"),
        P(("rep", "seq", "sub")), P("rep"), split,
    )
    out_specs = (split, P("rep", "mp", None), P("rep", None, "mp"))
    return jax.shard_map(body, mesh=mesh, in_specs=in_specs, out_specs=out_specs, check_vma=False)
```

profile of v0, /device:TPU:0, one launch (start us, length us, event | category | flops | bytes accessed | tf_op | source)
XLA Modules:
  0.0 130.8 jit_solution(1312982071594650051)
XLA Ops:
  0.6 1.9 %pack_keys_values.1 = (bf16[272,512]{1,0:T(8,128)(2,1)}, bf16[256,512]{1,0:T(8,128)(2,1)}) custom-call(bf16[256,512]{1,0:T(8,128)(2,1)} %keys.1, bf16[256,512]{1,0:T(8,128)(2,1)} %values.1, s32[1,256]{1,0:T(1,128)} %bitcast.12), custom_call_target="tpu_custom_call" | custom-call | bytes 1048576 | tf_op jit(solution)/shard_map/pack_keys_values/pallas_call | solution.py:73
  2.6 5.1 %collective-permute-start.3 = (bf16[272,512]{1,0:T(8,128)(2,1)}, bf16[272,512]{1,0:T(8,128)(2,1)S(1)}, u32[]{:S(2)}, u32[]{:S(2)}) collective-permute-start(bf16[272,512]{1,0:T(8,128)(2,1)} %get-tuple-element.24.own.refs_3_.refs_4_.refs_11_), channel_id=1, source_target_pairs={{0,4},{4,8},{8,12},{1,5},{5,9},{9,13},{2,6},{6,10},{10,14},{3,7},{... | collective-permute-start | bytes 835592 | tf_op jit(solution)/shard_map/ppermute | solution.py:512
  7.7 3.4 %down_project.1.after.refs_15_.refs_16_.refs_2_ = f32[24,256]{1,0:T(8,128)} custom-call(bf16[256,2560]{1,0:T(8,128)(2,1)} %refs_3_.1, bf16[128,2560]{1,0:T(8,128)(2,1)} %bitcast.11, s32[1,256]{1,0:T(1,128)} %bitcast.13, s32[16]{0:T(128)} %tenant_of.1), custom_call_target="tpu_custom_call" | custom-call | flops 167772160 | bytes 1966080 | tf_op jit(solution)/shard_map/down_project/pallas_call | solution.py:158
  11.0 2.8 %collective-permute-done.3.got.refs_5_.refs_6_.refs_12_ = bf16[272,512]{1,0:T(8,128)(2,1)S(1)} collective-permute-done((bf16[272,512]{1,0:T(8,128)(2,1)}, bf16[272,512]{1,0:T(8,128)(2,1)S(1)}, u32[]{:S(2)}, u32[]{:S(2)}) %collective-permute-start.3) | collective-permute-done | bytes 278560 | tf_op jit(solution)/shard_map/ppermute | solution.py:512
  13.9 0.1 relay_block.3
  14.0 1.3 collective-permute-start.5
  15.3 3.2 %collective-permute-start.4 = (bf16[272,512]{1,0:T(8,128)(2,1)S(1)}, bf16[272,512]{1,0:T(8,128)(2,1)S(1)}, u32[]{:S(2)}, u32[]{:S(2)}) collective-permute-start(bf16[272,512]{1,0:T(8,128)(2,1)S(1)} %collective-permute-done.3.got.refs_5_.refs_6_.refs_12_), channel_id=1, source_target_pairs={{0,1},{1,0},{2,3},{3,2},{4,5},{5,4},{6,7},{7,6},{8,9},{9,8},{10,11... | collective-permute-start | bytes 835592 | tf_op jit(solution)/shard_map/ppermute | solution.py:496
  18.5 3.5 %collective-permute-start = (bf16[256,512]{1,0:T(8,128)(2,1)S(1)}, bf16[256,512]{1,0:T(8,128)(2,1)S(1)}, u32[]{:S(2)}, u32[]{:S(2)}) collective-permute-start(bf16[256,512]{1,0:T(8,128)(2,1)S(1)} %copy-done.3), channel_id=1, source_target_pairs={{0,4},{4,8},{8,12},{1,5},{5,9},{9,13},{2,6},{6,10},{10,14},{3,7},{... | collective-permute-start | bytes 786440 | tf_op jit(solution)/shard_map/ppermute | solution.py:512
  21.9 1.6 %collective-permute-start.6 = (f32[24,256]{1,0:T(8,128)}, f32[24,256]{1,0:T(8,128)S(1)}, u32[]{:S(2)}, u32[]{:S(2)}) collective-permute-start(f32[24,256]{1,0:T(8,128)} %down_project.1.after.refs_15_.refs_16_.refs_2_), channel_id=1, source_target_pairs={{0,2},{2,0},{1,3},{3,1},{4,6},{6,4},{5,7},{7,5},{8,10},{10,8},{9,1... | collective-permute-start | bytes 73736 | tf_op jit(solution)/shard_map/ppermute | solution.py:496
  23.5 4.2 %collective-permute-done.got.refs_5_.refs_6_ = bf16[256,512]{1,0:T(8,128)(2,1)S(1)} collective-permute-done((bf16[256,512]{1,0:T(8,128)(2,1)S(1)}, bf16[256,512]{1,0:T(8,128)(2,1)S(1)}, u32[]{:S(2)}, u32[]{:S(2)}) %collective-permute-start) | collective-permute-done | bytes 262176 | tf_op jit(solution)/shard_map/ppermute | solution.py:512
  27.7 1.3 collective-permute-start.2
  29.1 3.3 %collective-permute-start.1 = (bf16[256,512]{1,0:T(8,128)(2,1)S(1)}, bf16[256,512]{1,0:T(8,128)(2,1)S(1)}, u32[]{:S(2)}, u32[]{:S(2)}) collective-permute-start(bf16[256,512]{1,0:T(8,128)(2,1)S(1)} %collective-permute-done.got.refs_5_.refs_6_), channel_id=1, source_target_pairs={{0,1},{1,0},{2,3},{3,2},{4,5},{5,4},{6,7},{7,6},{8,9},{9,8},{10,11... | collective-permute-start | bytes 786440 | tf_op jit(solution)/shard_map/ppermute | solution.py:496
  32.4 0.6 copy-done.13
  32.9 0.1 copy-done.8
  33.1 0.1 copy-done.9
  33.2 12.8 %attention.2 = (bf16[256,4096]{1,0:T(8,128)(2,1)}, bf16[64,2048]{1,0:T(8,128)(2,1)}, bf16[64,2048]{1,0:T(8,128)(2,1)}, f32[16,256]{1,0:T(8,128)}) custom-call(bf16[256,4096]{1,0:T(8,128)(2,1)} %refs_0_.3, bf16[256,4096]{1,0:T(8,128)(2,1)} %refs_1_.3, bf16[128,4096]{1,0:T(8,128)(2,1)} %bitcast.14, ...), custom_call_target="tpu_custom_call" | custom-call | flops 4294967296 | bytes 3145728 | tf_op jit(solution)/shard_map/attention/pallas_call | solution.py:342
  46.0 0.7 copy-done.11
  46.7 0.1 copy-done.12
  46.8 13.0 %attention.3 = (bf16[256,4096]{1,0:T(8,128)(2,1)}, bf16[64,2048]{1,0:T(8,128)(2,1)}, bf16[64,2048]{1,0:T(8,128)(2,1)}, f32[16,256]{1,0:T(8,128)}) custom-call(bf16[256,4096]{1,0:T(8,128)(2,1)} %refs_0_.3, bf16[256,4096]{1,0:T(8,128)(2,1)} %refs_1_.3, bf16[128,4096]{1,0:T(8,128)(2,1)} %bitcast.15, ...), custom_call_target="tpu_custom_call", output_to_operand_aliasing={{0}: (19, {})} | custom-call | flops 4294967296 | bytes 3145728 | tf_op jit(solution)/shard_map/attention/pallas_call | solution.py:342
  59.8 6.0 %collective-permute-start.9 = (bf16[64,2048]{1,0:T(8,128)(2,1)}, bf16[64,2048]{1,0:T(8,128)(2,1)S(1)}, u32[]{:S(2)}, u32[]{:S(2)}) collective-permute-start(bf16[64,2048]{1,0:T(8,128)(2,1)} %get-tuple-element.32), channel_id=1, source_target_pairs={{0,1},{1,0},{2,3},{3,2},{4,5},{5,4},{6,7},{7,6},{8,9},{9,8},{10,11... | collective-permute-start | bytes 786440 | tf_op jit(solution)/shard_map/ppermute | solution.py:496
  65.8 0.1 collective-permute-start.8
  65.9 1.5 %collective-permute-start.7 = (f32[16,256]{1,0:T(8,128)}, f32[16,256]{1,0:T(8,128)S(1)}, u32[]{:S(2)}, u32[]{:S(2)}) collective-permute-start(f32[16,256]{1,0:T(8,128)} %get-tuple-element.28.refs_0_), channel_id=1, source_target_pairs={{0,2},{2,0},{1,3},{3,1},{4,6},{6,4},{5,7},{7,5},{8,10},{10,8},{9,1... | collective-permute-start | bytes 49160 | tf_op jit(solution)/shard_map/ppermute | solution.py:496
  67.4 0.9 copy-done.6
  68.3 0.3 scatter_grads.2
  68.6 1.2 collective-permute-done.7.refs_1_
  69.8 0.7 copy-done.7
  70.5 1.1 split_grads.1
  71.7 0.1 collective-permute-start.10
  71.8 8.0 %collective-permute-start.17 = (bf16[16,4096]{1,0:T(8,128)(2,1)S(1)}, bf16[16,4096]{1,0:T(8,128)(2,1)S(1)}, u32[]{:S(2)}, u32[]{:S(2)}) collective-permute-start(bf16[16,4096]{1,0:T(8,128)(2,1)S(1)} %get-tuple-element.40), channel_id=1, source_target_pairs={{0,4},{4,8},{8,12},{12,0},{1,5},{5,9},{9,13},{13,1},{2,6},{6,10},{... | collective-permute-start | bytes 393224 | tf_op jit(solution)/shard_map/ppermute | solution.py:501
  79.7 4.6 %collective-permute-start.18 = (bf16[16,4096]{1,0:T(8,128)(2,1)S(1)}, bf16[16,4096]{1,0:T(8,128)(2,1)S(1)}, u32[]{:S(2)}, u32[]{:S(2)}) collective-permute-start(bf16[16,4096]{1,0:T(8,128)(2,1)S(1)} %get-tuple-element.41), channel_id=1, source_target_pairs={{0,8},{4,12},{8,0},{12,4},{1,9},{5,13},{9,1},{13,5},{2,10},{6,14},... | collective-permute-start | bytes 393224 | tf_op jit(solution)/shard_map/ppermute | solution.py:501
  84.4 2.8 %collective-permute-start.19 = (bf16[16,4096]{1,0:T(8,128)(2,1)S(1)}, bf16[16,4096]{1,0:T(8,128)(2,1)S(1)}, u32[]{:S(2)}, u32[]{:S(2)}) collective-permute-start(bf16[16,4096]{1,0:T(8,128)(2,1)S(1)} %get-tuple-element.42), channel_id=1, source_target_pairs={{0,12},{4,0},{8,4},{12,8},{1,13},{5,1},{9,5},{13,9},{2,14},{6,2},{... | collective-permute-start | bytes 393224 | tf_op jit(solution)/shard_map/ppermute | solution.py:501
  87.2 0.2 scatter_grads.3
  87.4 4.0 %collective-permute-done.18.refs_2_ = bf16[16,4096]{1,0:T(8,128)(2,1)S(1)} collective-permute-done((bf16[16,4096]{1,0:T(8,128)(2,1)S(1)}, bf16[16,4096]{1,0:T(8,128)(2,1)S(1)}, u32[]{:S(2)}, u32[]{:S(2)}) %collective-permute-start.18) | collective-permute-done | bytes 131104 | tf_op jit(solution)/shard_map/ppermute | solution.py:501
  91.5 0.1 sum_grads.3.refs_0_
  91.5 8.5 %collective-permute-start.22 = (bf16[16,4096]{1,0:T(8,128)(2,1)S(1)}, bf16[16,4096]{1,0:T(8,128)(2,1)S(1)}, u32[]{:S(2)}, u32[]{:S(2)}) collective-permute-start(bf16[16,4096]{1,0:T(8,128)(2,1)S(1)} %sum_grads.3.refs_0_), channel_id=1, source_target_pairs={{0,12},{4,0},{8,4},{12,8},{1,13},{5,1},{9,5},{13,9},{2,14},{6,2},{... | collective-permute-start | bytes 393224 | tf_op jit(solution)/shard_map/ppermute | solution.py:501
  100.0 0.6 collective-permute-start.20
  100.7 2.3 %collective-permute-start.12 = (bf16[16,2560]{1,0:T(8,128)(2,1)S(1)}, bf16[16,2560]{1,0:T(8,128)(2,1)S(1)}, u32[]{:S(2)}, u32[]{:S(2)}) collective-permute-start(bf16[16,2560]{1,0:T(8,128)(2,1)S(1)} %get-tuple-element.38), channel_id=1, source_target_pairs={{0,8},{4,12},{8,0},{12,4},{1,9},{5,13},{9,1},{13,5},{2,10},{6,14},... | collective-permute-start | bytes 245768 | tf_op jit(solution)/shard_map/ppermute | solution.py:501
  102.9 2.9 %collective-permute-start.13 = (bf16[16,2560]{1,0:T(8,128)(2,1)S(1)}, bf16[16,2560]{1,0:T(8,128)(2,1)S(1)}, u32[]{:S(2)}, u32[]{:S(2)}) collective-permute-start(bf16[16,2560]{1,0:T(8,128)(2,1)S(1)} %get-tuple-element.39), channel_id=1, source_target_pairs={{0,12},{4,0},{8,4},{12,8},{1,13},{5,1},{9,5},{13,9},{2,14},{6,2},{... | collective-permute-start | bytes 245768 | tf_op jit(solution)/shard_map/ppermute | solution.py:501
  105.9 8.8 %collective-permute-done.12.refs_2_ = bf16[16,2560]{1,0:T(8,128)(2,1)S(1)} collective-permute-done((bf16[16,2560]{1,0:T(8,128)(2,1)S(1)}, bf16[16,2560]{1,0:T(8,128)(2,1)S(1)}, u32[]{:S(2)}, u32[]{:S(2)}) %collective-permute-start.12) | collective-permute-done | bytes 81952 | tf_op jit(solution)/shard_map/ppermute | solution.py:501
  114.8 0.1 collective-permute-start.23
  114.9 4.6 %collective-permute-start.16 = (bf16[16,2560]{1,0:T(8,128)(2,1)S(1)}, bf16[16,2560]{1,0:T(8,128)(2,1)S(1)}, u32[]{:S(2)}, u32[]{:S(2)}) collective-permute-start(bf16[16,2560]{1,0:T(8,128)(2,1)S(1)} %sum_grads.2.refs_4_.refs_0_), channel_id=1, source_target_pairs={{0,12},{4,0},{8,4},{12,8},{1,13},{5,1},{9,5},{13,9},{2,14},{6,2},{... | collective-permute-start | bytes 245768 | tf_op jit(solution)/shard_map/ppermute | solution.py:501
  119.6 0.7 collective-permute-start.14
  120.2 2.2 %collective-permute-done.16.refs_3_ = bf16[16,2560]{1,0:T(8,128)(2,1)S(1)} collective-permute-done((bf16[16,2560]{1,0:T(8,128)(2,1)S(1)}, bf16[16,2560]{1,0:T(8,128)(2,1)S(1)}, u32[]{:S(2)}, u32[]{:S(2)}) %collective-permute-start.16) | collective-permute-done | bytes 81952 | tf_op jit(solution)/shard_map/ppermute | solution.py:501
  122.4 5.5 %collective-permute-done.15.refs_2_ = bf16[16,2560]{1,0:T(8,128)(2,1)S(1)} collective-permute-done((bf16[16,2560]{1,0:T(8,128)(2,1)S(1)}, bf16[16,2560]{1,0:T(8,128)(2,1)S(1)}, u32[]{:S(2)}, u32[]{:S(2)}) %collective-permute-start.15) | collective-permute-done | bytes 81952 | tf_op jit(solution)/shard_map/ppermute | solution.py:501
  127.9 0.1 collective-permute-start.24
  128.0 1.5 %finish_grads.3 = f32[128,4096]{1,0:T(8,128)} custom-call(bf16[64,4096]{1,0:T(8,128)(2,1)S(1)} %gather_grads.2.refs_0_, bf16[64,4096]{1,0:T(8,128)(2,1)S(1)} %collective-permute-done.23.refs_4_.refs_1_), custom_call_target="tpu_custom_call" | custom-call | flops 1048576 | bytes 2097152 | tf_op jit(solution)/shard_map/finish_grads/pallas_call | solution.py:369
  129.5 0.1 collective-permute-done.24.refs_1_
  129.6 1.1 finish_grads.2
  (45 shorter events, 0.3 us)
Async XLA Ops:
  2.6 11.3 %copy-start.1 = (bf16[272,512]{1,0:T(8,128)(2,1)S(1)}, bf16[272,512]{1,0:T(8,128)(2,1)}, u32[]{:S(2)}) copy-start(bf16[272,512]{1,0:T(8,128)(2,1)} %get-tuple-element.24.own.refs_3_.refs_4_.refs_11_) | copy-start | bytes 835588
  2.6 15.9 %copy-start.3 = (bf16[256,512]{1,0:T(8,128)(2,1)S(1)}, bf16[256,512]{1,0:T(8,128)(2,1)}, u32[]{:S(2)}) copy-start(bf16[256,512]{1,0:T(8,128)(2,1)} %get-tuple-element.23.own.refs_3_.refs_4_) | copy-start | bytes 786436
  2.6 11.3 %collective-permute-start.3 = (bf16[272,512]{1,0:T(8,128)(2,1)}, bf16[272,512]{1,0:T(8,128)(2,1)S(1)}, u32[]{:S(2)}, u32[]{:S(2)}) collective-permute-start(bf16[272,512]{1,0:T(8,128)(2,1)} %get-tuple-element.24.own.refs_3_.refs_4_.refs_11_), channel_id=1, source_target_pairs={{0,4},{4,8},{8,12},{1,5},{5,9},{9,13},{2,6},{6,10},{10,14},{3,7},{... | collective-permute-start | bytes 835592 | tf_op jit(solution)/shard_map/ppermute | solution.py:512
  13.9 18.5 %copy-start.2 = (bf16[272,512]{1,0:T(8,128)(2,1)}, bf16[272,512]{1,0:T(8,128)(2,1)S(1)}, u32[]{:S(2)}) copy-start(bf16[272,512]{1,0:T(8,128)(2,1)S(1)} %collective-permute-done.3.got.refs_5_.refs_6_.refs_12_) | copy-start | bytes 835588
  14.0 18.4 %collective-permute-start.5 = (bf16[272,512]{1,0:T(8,128)(2,1)S(1)}, bf16[272,512]{1,0:T(8,128)(2,1)S(1)}, u32[]{:S(2)}, u32[]{:S(2)}) collective-permute-start(bf16[272,512]{1,0:T(8,128)(2,1)S(1)} %relay_block.3), channel_id=1, source_target_pairs={{0,1},{1,4},{4,5},{5,8},{8,9},{9,12},{12,13},{2,3},{3,6},{6,7},{7,... | collective-permute-start | bytes 835592 | tf_op jit(solution)/shard_map/ppermute | solution.py:512
  15.3 17.1 %collective-permute-start.4 = (bf16[272,512]{1,0:T(8,128)(2,1)S(1)}, bf16[272,512]{1,0:T(8,128)(2,1)S(1)}, u32[]{:S(2)}, u32[]{:S(2)}) collective-permute-start(bf16[272,512]{1,0:T(8,128)(2,1)S(1)} %collective-permute-done.3.got.refs_5_.refs_6_.refs_12_), channel_id=1, source_target_pairs={{0,1},{1,0},{2,3},{3,2},{4,5},{5,4},{6,7},{7,6},{8,9},{9,8},{10,11... | collective-permute-start | bytes 835592 | tf_op jit(solution)/shard_map/ppermute | solution.py:496
  18.5 9.2 %collective-permute-start = (bf16[256,512]{1,0:T(8,128)(2,1)S(1)}, bf16[256,512]{1,0:T(8,128)(2,1)S(1)}, u32[]{:S(2)}, u32[]{:S(2)}) collective-permute-start(bf16[256,512]{1,0:T(8,128)(2,1)S(1)} %copy-done.3), channel_id=1, source_target_pairs={{0,4},{4,8},{8,12},{1,5},{5,9},{9,13},{2,6},{6,10},{10,14},{3,7},{... | collective-permute-start | bytes 786440 | tf_op jit(solution)/shard_map/ppermute | solution.py:512
  21.9 10.4 %collective-permute-start.6 = (f32[24,256]{1,0:T(8,128)}, f32[24,256]{1,0:T(8,128)S(1)}, u32[]{:S(2)}, u32[]{:S(2)}) collective-permute-start(f32[24,256]{1,0:T(8,128)} %down_project.1.after.refs_15_.refs_16_.refs_2_), channel_id=1, source_target_pairs={{0,2},{2,0},{1,3},{3,1},{4,6},{6,4},{5,7},{7,5},{8,10},{10,8},{9,1... | collective-permute-start | bytes 73736 | tf_op jit(solution)/shard_map/ppermute | solution.py:496
  27.7 18.3 %copy-start.4 = (bf16[256,512]{1,0:T(8,128)(2,1)}, bf16[256,512]{1,0:T(8,128)(2,1)S(1)}, u32[]{:S(2)}) copy-start(bf16[256,512]{1,0:T(8,128)(2,1)S(1)} %collective-permute-done.got.refs_5_.refs_6_) | copy-start | bytes 786436
  27.7 18.2 %collective-permute-start.2 = (bf16[256,512]{1,0:T(8,128)(2,1)S(1)}, bf16[256,512]{1,0:T(8,128)(2,1)S(1)}, u32[]{:S(2)}, u32[]{:S(2)}) collective-permute-start(bf16[256,512]{1,0:T(8,128)(2,1)S(1)} %relay_block.2), channel_id=1, source_target_pairs={{0,1},{1,4},{4,5},{5,8},{8,9},{9,12},{12,13},{2,3},{3,6},{6,7},{7,... | collective-permute-start | bytes 786440 | tf_op jit(solution)/shard_map/ppermute | solution.py:512
  29.1 17.0 %collective-permute-start.1 = (bf16[256,512]{1,0:T(8,128)(2,1)S(1)}, bf16[256,512]{1,0:T(8,128)(2,1)S(1)}, u32[]{:S(2)}, u32[]{:S(2)}) collective-permute-start(bf16[256,512]{1,0:T(8,128)(2,1)S(1)} %collective-permute-done.got.refs_5_.refs_6_), channel_id=1, source_target_pairs={{0,1},{1,0},{2,3},{3,2},{4,5},{5,4},{6,7},{7,6},{8,9},{9,8},{10,11... | collective-permute-start | bytes 786440 | tf_op jit(solution)/shard_map/ppermute | solution.py:496
  32.3 0.6 copy-start.13
  32.3 0.7 copy-start.8
  32.4 0.8 copy-start.9
  46.0 0.7 copy-start.11
  46.0 0.8 copy-start.12
  46.8 19.0 %copy-start.10 = (bf16[64,2048]{1,0:T(8,128)(2,1)S(1)}, bf16[64,2048]{1,0:T(8,128)(2,1)}, u32[]{:S(2)}) copy-start(bf16[64,2048]{1,0:T(8,128)(2,1)} %get-tuple-element.30) | copy-start | bytes 786436
  46.8 20.6 %copy-start.5 = (bf16[64,2048]{1,0:T(8,128)(2,1)S(1)}, bf16[64,2048]{1,0:T(8,128)(2,1)}, u32[]{:S(2)}) copy-start(bf16[64,2048]{1,0:T(8,128)(2,1)} %get-tuple-element.29.refs_0_) | copy-start | bytes 786436
  46.8 23.0 %copy-start = (bf16[256,2560]{1,0:T(8,128)(2,1)S(1)}, bf16[256,2560]{1,0:T(8,128)(2,1)}, u32[]{:S(2)}) copy-start(bf16[256,2560]{1,0:T(8,128)(2,1)} %refs_3_.1) | copy-start | bytes 3932164
  59.8 7.6 %collective-permute-start.9 = (bf16[64,2048]{1,0:T(8,128)(2,1)}, bf16[64,2048]{1,0:T(8,128)(2,1)S(1)}, u32[]{:S(2)}, u32[]{:S(2)}) collective-permute-start(bf16[64,2048]{1,0:T(8,128)(2,1)} %get-tuple-element.32), channel_id=1, source_target_pairs={{0,1},{1,0},{2,3},{3,2},{4,5},{5,4},{6,7},{7,6},{8,9},{9,8},{10,11... | collective-permute-start | bytes 786440 | tf_op jit(solution)/shard_map/ppermute | solution.py:496
  65.8 1.6 %collective-permute-start.8 = (bf16[64,2048]{1,0:T(8,128)(2,1)S(1)}, bf16[64,2048]{1,0:T(8,128)(2,1)S(1)}, u32[]{:S(2)}, u32[]{:S(2)}) collective-permute-start(bf16[64,2048]{1,0:T(8,128)(2,1)S(1)} %copy-done.10), channel_id=1, source_target_pairs={{0,1},{1,0},{2,3},{3,2},{4,5},{5,4},{6,7},{7,6},{8,9},{9,8},{10,11... | collective-permute-start | bytes 786440 | tf_op jit(solution)/shard_map/ppermute | solution.py:496
  65.9 3.9 %collective-permute-start.7 = (f32[16,256]{1,0:T(8,128)}, f32[16,256]{1,0:T(8,128)S(1)}, u32[]{:S(2)}, u32[]{:S(2)}) collective-permute-start(f32[16,256]{1,0:T(8,128)} %get-tuple-element.28.refs_0_), channel_id=1, source_target_pairs={{0,2},{2,0},{1,3},{3,1},{4,6},{6,4},{5,7},{7,5},{8,10},{10,8},{9,1... | collective-permute-start | bytes 49160 | tf_op jit(solution)/shard_map/ppermute | solution.py:496
  67.4 1.0 copy-start.6
  69.8 0.7 copy-start.7
  71.7 15.5 %collective-permute-start.10 = (bf16[64,2560]{1,0:T(8,128)(2,1)S(1)}, bf16[64,2560]{1,0:T(8,128)(2,1)S(1)}, u32[]{:S(2)}, u32[]{:S(2)}) collective-permute-start(bf16[64,2560]{1,0:T(8,128)(2,1)S(1)} %get-tuple-element.35), channel_id=1, source_target_pairs={{0,1},{1,0},{2,3},{3,2},{4,5},{5,4},{6,7},{7,6},{8,9},{9,8},{10,11... | collective-permute-start | bytes 983048 | tf_op jit(solution)/shard_map/ppermute | solution.py:496
  71.8 15.7 %collective-permute-start.17 = (bf16[16,4096]{1,0:T(8,128)(2,1)S(1)}, bf16[16,4096]{1,0:T(8,128)(2,1)S(1)}, u32[]{:S(2)}, u32[]{:S(2)}) collective-permute-start(bf16[16,4096]{1,0:T(8,128)(2,1)S(1)} %get-tuple-element.40), channel_id=1, source_target_pairs={{0,4},{4,8},{8,12},{12,0},{1,5},{5,9},{9,13},{13,1},{2,6},{6,10},{... | collective-permute-start | bytes 393224 | tf_op jit(solution)/shard_map/ppermute | solution.py:501
  79.7 11.7 %collective-permute-start.18 = (bf16[16,4096]{1,0:T(8,128)(2,1)S(1)}, bf16[16,4096]{1,0:T(8,128)(2,1)S(1)}, u32[]{:S(2)}, u32[]{:S(2)}) collective-permute-start(bf16[16,4096]{1,0:T(8,128)(2,1)S(1)} %get-tuple-element.41), channel_id=1, source_target_pairs={{0,8},{4,12},{8,0},{12,4},{1,9},{5,13},{9,1},{13,5},{2,10},{6,14},... | collective-permute-start | bytes 393224 | tf_op jit(solution)/shard_map/ppermute | solution.py:501
  84.4 7.1 %collective-permute-start.19 = (bf16[16,4096]{1,0:T(8,128)(2,1)S(1)}, bf16[16,4096]{1,0:T(8,128)(2,1)S(1)}, u32[]{:S(2)}, u32[]{:S(2)}) collective-permute-start(bf16[16,4096]{1,0:T(8,128)(2,1)S(1)} %get-tuple-element.42), channel_id=1, source_target_pairs={{0,12},{4,0},{8,4},{12,8},{1,13},{5,1},{9,5},{13,9},{2,14},{6,2},{... | collective-permute-start | bytes 393224 | tf_op jit(solution)/shard_map/ppermute | solution.py:501
  87.4 15.6 %collective-permute-start.11 = (bf16[16,2560]{1,0:T(8,128)(2,1)S(1)}, bf16[16,2560]{1,0:T(8,128)(2,1)S(1)}, u32[]{:S(2)}, u32[]{:S(2)}) collective-permute-start(bf16[16,2560]{1,0:T(8,128)(2,1)S(1)} %get-tuple-element.37), channel_id=1, source_target_pairs={{0,4},{4,8},{8,12},{12,0},{1,5},{5,9},{9,13},{13,1},{2,6},{6,10},{... | collective-permute-start | bytes 245768 | tf_op jit(solution)/shard_map/ppermute | solution.py:501
  91.5 23.2 %collective-permute-start.22 = (bf16[16,4096]{1,0:T(8,128)(2,1)S(1)}, bf16[16,4096]{1,0:T(8,128)(2,1)S(1)}, u32[]{:S(2)}, u32[]{:S(2)}) collective-permute-start(bf16[16,4096]{1,0:T(8,128)(2,1)S(1)} %sum_grads.3.refs_0_), channel_id=1, source_target_pairs={{0,12},{4,0},{8,4},{12,8},{1,13},{5,1},{9,5},{13,9},{2,14},{6,2},{... | collective-permute-start | bytes 393224 | tf_op jit(solution)/shard_map/ppermute | solution.py:501
  100.0 14.8 %collective-permute-start.21 = (bf16[16,4096]{1,0:T(8,128)(2,1)S(1)}, bf16[16,4096]{1,0:T(8,128)(2,1)S(1)}, u32[]{:S(2)}, u32[]{:S(2)}) collective-permute-start(bf16[16,4096]{1,0:T(8,128)(2,1)S(1)} %sum_grads.3.refs_0_), channel_id=1, source_target_pairs={{0,8},{4,12},{8,0},{12,4},{1,9},{5,13},{9,1},{13,5},{2,10},{6,14},... | collective-permute-start | bytes 393224 | tf_op jit(solution)/shard_map/ppermute | solution.py:501
  100.0 14.8 %collective-permute-start.20 = (bf16[16,4096]{1,0:T(8,128)(2,1)S(1)}, bf16[16,4096]{1,0:T(8,128)(2,1)S(1)}, u32[]{:S(2)}, u32[]{:S(2)}) collective-permute-start(bf16[16,4096]{1,0:T(8,128)(2,1)S(1)} %sum_grads.3.refs_0_), channel_id=1, source_target_pairs={{0,4},{4,8},{8,12},{12,0},{1,5},{5,9},{9,13},{13,1},{2,6},{6,10},{... | collective-permute-start | bytes 393224 | tf_op jit(solution)/shard_map/ppermute | solution.py:501
  100.7 14.0 %collective-permute-start.12 = (bf16[16,2560]{1,0:T(8,128)(2,1)S(1)}, bf16[16,2560]{1,0:T(8,128)(2,1)S(1)}, u32[]{:S(2)}, u32[]{:S(2)}) collective-permute-start(bf16[16,2560]{1,0:T(8,128)(2,1)S(1)} %get-tuple-element.38), channel_id=1, source_target_pairs={{0,8},{4,12},{8,0},{12,4},{1,9},{5,13},{9,1},{13,5},{2,10},{6,14},... | collective-permute-start | bytes 245768 | tf_op jit(solution)/shard_map/ppermute | solution.py:501
  102.9 11.8 %collective-permute-start.13 = (bf16[16,2560]{1,0:T(8,128)(2,1)S(1)}, bf16[16,2560]{1,0:T(8,128)(2,1)S(1)}, u32[]{:S(2)}, u32[]{:S(2)}) collective-permute-start(bf16[16,2560]{1,0:T(8,128)(2,1)S(1)} %get-tuple-element.39), channel_id=1, source_target_pairs={{0,12},{4,0},{8,4},{12,8},{1,13},{5,1},{9,5},{13,9},{2,14},{6,2},{... | collective-permute-start | bytes 245768 | tf_op jit(solution)/shard_map/ppermute | solution.py:501
  114.8 13.0 %collective-permute-start.23 = (bf16[64,4096]{1,0:T(8,128)(2,1)S(1)}, bf16[64,4096]{1,0:T(8,128)(2,1)S(1)}, u32[]{:S(2)}, u32[]{:S(2)}) collective-permute-start(bf16[64,4096]{1,0:T(8,128)(2,1)S(1)} %gather_grads.2.refs_0_), channel_id=1, source_target_pairs={{0,1},{1,0},{2,3},{3,2},{4,5},{5,4},{6,7},{7,6},{8,9},{9,8},{10,11... | collective-permute-start | bytes 1572872 | tf_op jit(solution)/shard_map/ppermute | solution.py:496
  114.9 7.5 %collective-permute-start.16 = (bf16[16,2560]{1,0:T(8,128)(2,1)S(1)}, bf16[16,2560]{1,0:T(8,128)(2,1)S(1)}, u32[]{:S(2)}, u32[]{:S(2)}) collective-permute-start(bf16[16,2560]{1,0:T(8,128)(2,1)S(1)} %sum_grads.2.refs_4_.refs_0_), channel_id=1, source_target_pairs={{0,12},{4,0},{8,4},{12,8},{1,13},{5,1},{9,5},{13,9},{2,14},{6,2},{... | collective-permute-start | bytes 245768 | tf_op jit(solution)/shard_map/ppermute | solution.py:501
  119.6 8.3 %collective-permute-start.15 = (bf16[16,2560]{1,0:T(8,128)(2,1)S(1)}, bf16[16,2560]{1,0:T(8,128)(2,1)S(1)}, u32[]{:S(2)}, u32[]{:S(2)}) collective-permute-start(bf16[16,2560]{1,0:T(8,128)(2,1)S(1)} %sum_grads.2.refs_4_.refs_0_), channel_id=1, source_target_pairs={{0,8},{4,12},{8,0},{12,4},{1,9},{5,13},{9,1},{13,5},{2,10},{6,14},... | collective-permute-start | bytes 245768 | tf_op jit(solution)/shard_map/ppermute | solution.py:501
  119.6 8.3 %collective-permute-start.14 = (bf16[16,2560]{1,0:T(8,128)(2,1)S(1)}, bf16[16,2560]{1,0:T(8,128)(2,1)S(1)}, u32[]{:S(2)}, u32[]{:S(2)}) collective-permute-start(bf16[16,2560]{1,0:T(8,128)(2,1)S(1)} %sum_grads.2.refs_4_.refs_0_), channel_id=1, source_target_pairs={{0,4},{4,8},{8,12},{12,0},{1,5},{5,9},{9,13},{13,1},{2,6},{6,10},{... | collective-permute-start | bytes 245768 | tf_op jit(solution)/shard_map/ppermute | solution.py:501
  127.9 1.7 %collective-permute-start.24 = (bf16[64,2560]{1,0:T(8,128)(2,1)S(1)}, bf16[64,2560]{1,0:T(8,128)(2,1)S(1)}, u32[]{:S(2)}, u32[]{:S(2)}) collective-permute-start(bf16[64,2560]{1,0:T(8,128)(2,1)S(1)} %gather_grads.3.refs_0_), channel_id=1, source_target_pairs={{0,1},{1,0},{2,3},{3,2},{4,5},{5,4},{6,7},{7,6},{8,9},{9,8},{10,11... | collective-permute-start | bytes 983048 | tf_op jit(solution)/shard_map/ppermute | solution.py:496
where the time goes:
time: 131 us
  starting transfers between devices  62.1 us (47%)
  Pallas kernels  35.6 us (27%)
  waiting for transfers between devices  28.9 us (22%)
  local copies, waits for them, and re-layouts  3.25 us (2%)
    ppermute x12, starting transfers between devices, rotate_over(): return lax.ppermute(block, axis, [(i, (i + d) % size) for i in range(size)])  35.1 us
    pallas_call x2, Pallas kernels, attention(): pl.pallas_call(kernel, grid=(count,), out_shape=[jax.ShapeDtypeStruct((ro...  25.8 us
    ppermute x12, waiting for transfers between devices, rotate_over(): return lax.ppermute(block, axis, [(i, (i + d) % size) for i in range(size)])  20.5 us
    ppermute x9, starting transfers between devices, swap_over(): return lax.ppermute(block, axis, [(0, 1), (1, 0)])  15.8 us
    ppermute x4, starting transfers between devices, shift_over(): return lax.ppermute(block, axis, [(i, i + 1) for i in range(size - 1)])  11.2 us
    ppermute x4, waiting for transfers between devices, shift_over(): return lax.ppermute(block, axis, [(i, i + 1) for i in range(size - 1)])  7.01 us
    pallas_call x9, Pallas kernels, small_call(): pl.pallas_call(lambda *refs: kernel(*refs[:count], *refs[len(given):outs]...  4.36 us
    pallas_call x1, Pallas kernels, down_project(): pl.pallas_call(functools.partial(down_kernel, tenants, rank), out_shape=j...  3.36 us
  transfers between devices with their start and end apart: 25, of which 8 were waited for; matrix products, arithmetic and copies ran while one was open for 0% of the time, Pallas kernels for 14%

commit v1 on v0

--- a/solution.py
+++ b/solution.py
@@ -41,45 +41,39 @@
     return copies
 
 
-def pack_kernel(counts, keys, values, doc, *rest):
-    outs, (ids, blocks, tail, sems) = rest[: len(counts)], rest[len(counts) :]
+def pack_kernel(keys, values, doc, out, ids, blocks, sems):
     rows, width = keys.shape
     loads = fetch(
-        [(doc, ids), (keys, blocks.at[0]), (values, blocks.at[1])], sems.at[pl.ds(0, 3)]
+        [
+            (doc, ids),
+            (keys, blocks.at[pl.ds(0, rows), pl.ds(0, width)]),
+            (values, blocks.at[pl.ds(0, rows), pl.ds(width, width)]),
+        ],
+        sems.at[pl.ds(0, 3)],
     )
     loads[0].wait()
-    tail[...] = jnp.zeros_like(tail)
-    tail[:, 0:rows] = jnp.broadcast_to((ids[...] + 1).astype(jnp.float32), (TAIL, rows)).astype(
+    blocks[rows:, :] = jnp.zeros((TAIL, 2 * width), jnp.bfloat16)
+    blocks[rows:, 0:rows] = jnp.broadcast_to((ids[...] + 1).astype(jnp.float32), (TAIL, rows)).astype(
         jnp.bfloat16
     )
-    pairs, first = [(tail, outs[0].at[pl.ds(rows, TAIL), :])], 0
-    for count, out in zip(counts, outs):
-        for half in range(2):
-            source = blocks.at[half, :, pl.ds(first * HEAD, count * HEAD)]
-            pairs.append((source, out.at[pl.ds(0, rows), pl.ds(half * count * HEAD, count * HEAD)]))
-        first += count
     loads[1].wait()
     loads[2].wait()
-    for copy in fetch(pairs, sems.at[pl.ds(3, len(pairs))]):
-        copy.wait()
-
-
-def pack(keys, values, doc, counts):
+    for store in fetch([(blocks, out)], sems.at[pl.ds(3, 1)]):
+        store.wait()
+
+
+def pack(keys, values, doc):
     rows, width = keys.shape
-    shapes = [
-        jax.ShapeDtypeStruct((rows + (0 if i else TAIL), 2 * count * HEAD), jnp.bfloat16)
-        for i, count in enumerate(counts)
-    ]
+    shape = (rows + TAIL, 2 * width)
     return pl.pallas_call(
-        functools.partial(pack_kernel, counts),
-        out_shape=shapes,
+        pack_kernel,
+        out_shape=jax.ShapeDtypeStruct(shape, jnp.bfloat16),
         in_specs=[ANY] * 3,
-        out_specs=[ANY] * len(counts),
+        out_specs=ANY,
         scratch_shapes=[
             pltpu.VMEM((1, rows), jnp.int32),
-            pltpu.VMEM((2, rows, width), jnp.bfloat16),
-            pltpu.VMEM((TAIL, shapes[0].shape[1]), jnp.bfloat16),
-            pltpu.SemaphoreType.DMA((4 + 2 * len(counts),)),
+            pltpu.VMEM(shape, jnp.bfloat16),
+            pltpu.SemaphoreType.DMA((4,)),
         ],
         compiler_params=params(VMEM_MOST),
         cost_estimate=pl.CostEstimate(flops=0, bytes_accessed=8 * rows * width, transcendentals=0),
@@ -87,7 +81,8 @@
     )(keys, values, doc)
 
 
-def relay_kernel(own, got, after, out, held, sems):
+def relay_kernel(own, got, after, *rest):
+    outs, held, sems = rest[:-3], rest[-2], rest[-1]
     sub = lax.axis_index("sub")
 
     def move(source):
@@ -103,22 +98,39 @@
     def _():
         move(got)
 
-    store = pltpu.make_async_copy(held, out, sems.at[1])
-    store.start()
-    store.wait()
-
-
-def relay(own, got, after):
-    return pl.pallas_call(
+    width = held.shape[1] // 2
+    part = width // len(outs)
+    pairs = []
+    for c, out in enumerate(outs):
+        for half in range(2):
+            pairs.append(
+                (
+                    held.at[:, pl.ds(half * width + c * part, part)],
+                    out.at[:, pl.ds(half * part, part)],
+                )
+            )
+    for store in fetch(pairs, sems.at[pl.ds(1, len(pairs))]):
+        store.wait()
+
+
+def relay(own, got, after, chunks):
+    rows, width = own.shape
+    *parts, got = pl.pallas_call(
         relay_kernel,
-        out_shape=jax.ShapeDtypeStruct(own.shape, own.dtype),
+        out_shape=[jax.ShapeDtypeStruct((rows, width // chunks), own.dtype)] * chunks
+        + [jax.ShapeDtypeStruct(own.shape, own.dtype)],
         in_specs=[ANY, ANY, ANY],
-        out_specs=ANY,
-        scratch_shapes=[pltpu.VMEM(own.shape, own.dtype), pltpu.SemaphoreType.DMA((2,))],
+        out_specs=[ANY] * (chunks + 1),
+        input_output_aliases={1: chunks},
+        scratch_shapes=[
+            pltpu.VMEM(own.shape, own.dtype),
+            pltpu.SemaphoreType.DMA((1 + 2 * chunks,)),
+        ],
         compiler_params=params(),
         cost_estimate=pl.CostEstimate(flops=0, bytes_accessed=4 * own.size, transcendentals=0),
         name="relay_block",
     )(own, got, after)
+    return parts, got
 
 
 def selector_of(owner, tenants, rank):
@@ -180,9 +192,9 @@
     return info[rank : rank + 1, :].astype(jnp.int32)
 
 
-def attention(chunk, chunks, base, grad, up, blocks, first, info, terms, before, tenants, rank):
+def attention(chunk, chunks, base, grad, up, blocks, with_ids, info, terms, before, tenants, rank):
     rows, width = base.shape
-    count = blocks[0].shape[1] // (2 * HEAD)
+    count = blocks[3].shape[1] // (2 * HEAD)
     window = (REACH + 1) * rows
     tall = tenants * rank
     half = tall // 2
@@ -193,15 +205,15 @@
     offset = chunk * count
     wide = lambda r: pl.BlockSpec((r, span), lambda i: (0, i + offset))
     narrow = pl.BlockSpec((half, span), lambda i: (0, i))
-    keys = pl.BlockSpec((rows, HEAD), lambda i: (0, i))
-    values = pl.BlockSpec((rows, HEAD), lambda i: (0, i + count))
+    column = lambda at: pl.BlockSpec((rows, HEAD), lambda i: (0, i + at))
     ids = pl.BlockSpec((TAIL, rows), lambda i: (rows // TAIL, 0))
     same = lambda a: pl.BlockSpec(a.shape, lambda i: (0, 0))
     operands, specs = [base, grad, up], [wide(rows), wide(rows), wide(tall)]
     for block in blocks:
         operands += [block, block]
-        specs += [keys, values]
-    operands += [*first, info, *terms]
+        skip = 0 if block is blocks[3] else offset
+        specs += [column(skip), column(skip + block.shape[1] // (2 * HEAD))]
+    operands += [*with_ids, info, *terms]
     specs += [ids] * 4 + [same(info)] * 3
     if before is not None:
         operands += [before[1], before[0]]
@@ -214,7 +226,8 @@
         bottle=pltpu.VMEM((rows, tall), jnp.bfloat16),
         bottle_t=pltpu.VMEM((tall, rows), jnp.bfloat16),
         bias=pltpu.VMEM((window, rows), jnp.float32),
-        query=pltpu.VMEM((rows, span), jnp.bfloat16),
+        query=pltpu.VMEM((span, rows), jnp.bfloat16),
+        gt=pltpu.VMEM((span, rows), jnp.bfloat16),
         gquery=pltpu.VMEM((span, rows), jnp.bfloat16),
         scores=pltpu.VMEM((pair, window, rows), jnp.float32),
         part=pltpu.VMEM((tall, span), jnp.bfloat16),
@@ -228,7 +241,9 @@
         out, keep, send, projected = refs[len(operands) : len(operands) + 4]
         r = dict(zip(held, refs[len(operands) + 4 :]))
         kw, vw, kt, vt = (r[n] for n in ("kw", "vw", "kt", "vt"))
-        bias, query, gquery, scores = (r[n] for n in ("bias", "query", "gquery", "scores"))
+        bias, query, gt, gquery, scores = (
+            r[n] for n in ("bias", "query", "gt", "gquery", "scores")
+        )
         sub = lax.axis_index("sub")
         step = pl.program_id(0)
 
@@ -279,19 +294,18 @@
             place(2, *kv[6:8])
             place(0, *kv[4:6])
 
-        query[...] = (
-            base[...].astype(jnp.float32) + LIFT * nn(r["bottle"][...], up[...])
-        ).astype(jnp.bfloat16)
-        ones = jnp.ones((TAIL, 2 * HEAD), jnp.bfloat16)
+        lift = LIFT * nn(r["bottle"][...], up[...])
+        query[...] = (base[...].astype(jnp.float32) + lift).astype(jnp.bfloat16).T
+        gt[...] = grad[...].T
 
         def run(reached, numbers):
             chunks = [slice(c * rows, (c + 1) * rows) for c in range(REACH - reached, REACH + 1)]
             spans = [pl.ds(pl.multiple_of(h * HEAD, HEAD), HEAD) for h in numbers]
             peaks = []
             for i, span_i in enumerate(spans):
-                q, peak = query[:, span_i], None
+                q, peak = query[span_i, :], None
                 for c in chunks:
-                    s = nt(kw[c, :], q) + bias[c, :]
+                    s = nn(kw[c, :], q) + bias[c, :]
                     scores[i, c, :] = s
                     top = jnp.max(s, axis=0, keepdims=True)
                     peak = top if peak is None else jnp.maximum(peak, top)
@@ -305,17 +319,15 @@
                     o = nn(vt[:, c], w.astype(jnp.bfloat16))
                     total = o if total is None else total + o
                 inverse = 1.0 / total[HEAD : HEAD + 1, :]
-                attn = (total[0:HEAD, :] * inverse).astype(jnp.bfloat16).T
-                out[:, span_i] = attn
-                product = grad[:, span_i].astype(jnp.float32) * attn.astype(jnp.float32)
-                high = product.astype(jnp.bfloat16)
-                low = (product - high.astype(jnp.float32)).astype(jnp.bfloat16)
-                rowdots.append(nt(ones, jnp.concatenate([high, low], axis=1))[0:1, :])
+                attn = (total[0:HEAD, :] * inverse).astype(jnp.bfloat16)
+                out[:, span_i] = attn.T
+                product = gt[span_i, :].astype(jnp.float32) * attn.astype(jnp.float32)
+                rowdots.append(jnp.sum(product, axis=0, keepdims=True))
                 inverses.append(inverse)
             for i, span_i in enumerate(spans):
-                g, moved = grad[:, span_i], None
+                g, moved = gt[span_i, :], None
                 for c in chunks:
-                    dprob = nt(vw[c, :], g)
+                    dprob = nn(vw[c, :], g)
                     ds = (scores[i, c, :] * (dprob - rowdots[i])).astype(jnp.bfloat16)
                     dq = nn(kt[:, c], ds)
                     moved = dq if moved is None else moved + dq
@@ -447,20 +459,32 @@
     )
 
 
-def finish_kernel(half_ref, other_ref, out):
+def finish_kernel(count, *refs):
+    grad_b, grad_a = refs[2 * count :]
     sub = lax.axis_index("sub")
-    half = half_ref.shape[0]
+    half, wide = refs[0].shape[0], grad_b.shape[1]
     here = pl.ds(pl.multiple_of(sub * half, half), half)
     there = pl.ds(pl.multiple_of((1 - sub) * half, half), half)
-    out[here, :] = half_ref[...].astype(jnp.float32)
-    out[there, :] = other_ref[...].astype(jnp.float32)
-
-
-def finish(half, other):
-    rows, width = half.shape
+    for at, group in ((here, refs[0 : 2 * count : 2]), (there, refs[1 : 2 * count : 2])):
+        col = 0
+        for ref in group:
+            width = ref.shape[1]
+            first = min(width, wide - col)
+            grad_b[at, col : col + first] = ref[:, 0:first].astype(jnp.float32)
+            if first < width:
+                grad_a[at, :] = ref[:, first:].astype(jnp.float32)
+            col += width
+
+
+def finish(pairs, wide):
+    rows, width = pairs[0][0].shape[0] * 2, sum(half.shape[1] for half, _ in pairs)
     return small_call(
-        finish_kernel, "finish_grads", jax.ShapeDtypeStruct((2 * rows, width), jnp.float32),
-        half, other,
+        functools.partial(finish_kernel, len(pairs)), "finish_grads",
+        [
+            jax.ShapeDtypeStruct((rows, wide), jnp.float32),
+            jax.ShapeDtypeStruct((rows, width - wide), jnp.float32),
+        ],
+        *[block for pair in pairs for block in pair],
     )
 
 
@@ -524,44 +548,47 @@
     up = adapter_up.reshape(tall, up_width)
     key_heads = base_keys.shape[1] // HEAD
     chunks = 2 if key_heads % 2 == 0 else 1
-    counts = (key_heads // chunks,) * chunks
     size = lax.axis_size("seq")
-    by_hand = tall % (2 * TAIL * size) == 0
-
-    own = pack(base_keys, base_values, doc, counts)
-    two = [shift_over(block, "seq") for block in own]
+    by_hand = chunks == 2 and tall % (2 * TAIL * size) == 0
+
+    own = pack(base_keys, base_values, doc)
+    two = shift_over(own, "seq")
     info = down_project(normed_inputs, adapter, doc, document_tenant, tenants, rank)
-    swapped = [swap_over(block, "sub") for block in two]
-    passed = [shift_over(relay(o, t, info), ("seq", "sub")) for o, t in zip(own, two)]
     terms = terms_over(info, "mp")
-    first = (own[0], two[0], swapped[0], passed[0])
+    parts, two = relay(own, two, terms[1], chunks)
+    passed = [shift_over(part, ("seq", "sub")) for part in parts]
+    swapped = swap_over(two, "sub")
+    with_ids = (own, two, swapped, passed[0])
 
     state, pairs = None, []
     for c in range(chunks):
         out, keep, send, gdown = attention(
-            c, chunks, base_queries, output_gradient, up,
-            (own[c], two[c], swapped[c], passed[c]), first, info, terms, state, tenants, rank,
+            c, chunks, base_queries, output_gradient, up, (own, two, swapped, passed[c]),
+            with_ids, info, terms, state, tenants, rank,
         )
         state = (out, gdown)
         pairs.append((keep, send))
-    one, other = terms_over(gdown, "mp")
     if by_hand:
-        shards_b = scatter(*[(keep, swap_over(send, "sub")) for keep, send in pairs])
-        keep, send = small_call(
+        (keep, send), (keep_late, send_late) = pairs
+        one, other = terms_over(gdown, "mp")
+        pieces = exchange(scatter((keep, swap_over(send, "sub")), after=[keep_late]))
+        early = add_up(pieces)
+        keep_a, send_a = small_call(
             functools.partial(split_kernel, tenants, rank), "split_grads", halves_of(tall, width),
-            one, other, info, normed_inputs, after=shards_b[:1],
+            one, other, info, normed_inputs, after=pieces[1:2],
         )
-        pieces_b = exchange(shards_b)
-        shards_a = scatter((keep, swap_over(send, "sub")))
-        pieces_a = exchange(shards_a)
-        all_b = spread(add_up(pieces_b, after=shards_a[:1]))
-        sum_a = add_up(pieces_a)
-        half_b = gather(all_b, after=[sum_a])
-        other_b = swap_over(half_b, "sub")
-        half_a = gather(spread(sum_a), after=[other_b])
-        grad_b = finish(half_b, other_b)
-        grad_a = finish(half_a, swap_over(half_a, "sub"))
+        shards = scatter(
+            (keep_late, swap_over(send_late, "sub")), (keep_a, swap_over(send_a, "sub")), after=[early]
+        )
+        late = add_up(exchange(shards))
+        half_early = gather(spread(early), after=[late])
+        other_early = swap_over(half_early, "sub")
+        half_late = gather(spread(late), after=[other_early])
+        grad_b, grad_a = finish(
+            [(half_early, other_early), (half_late, swap_over(half_late, "sub"))], up_width
+        )
     else:
+        one, other = terms_over(gdown, "mp")
         part_a = small_call(
             functools.partial(grad_a_kernel, tenants, rank), "grad_a_part",
             jax.ShapeDtypeStruct((tall, width), jnp.bfloat16), one, other, info, normed_inputs,

time: 131 us -> 122 us (0.931); the launches traced: 131 us -> 120 us
  starting transfers between devices: 62.1 us -> 52.3 us
  Pallas kernels: 35.6 us -> 31.4 us
  waiting for transfers between devices: 28.9 us -> 32.4 us
    ppermute x9 -> x8, starting transfers between devices: 15.8 us -> 7.89 us  [swap_over(): return lax.ppermute(block, axis, [(0, 1), (1, 0)])]
    ppermute x9 -> x8, waiting for transfers between devices: 1.39 us -> 6.99 us  [swap_over(): return lax.ppermute(block, axis, [(0, 1), (1, 0)])]
    pallas_call x2, Pallas kernels: 25.8 us -> 23 us  [attention(): pl.pallas_call(kernel, grid=(count,), out_shape=[jax.ShapeDtypeStruct((ro...]
    ppermute x4 -> x3, waiting for transfers between devices: 7.01 us -> 4.67 us  [shift_over(): return lax.ppermute(block, axis, [(i, i + 1) for i in range(size - 1)])]
    ppermute x12, starting transfers between devices: 35.1 us -> 33 us  [rotate_over(): return lax.ppermute(block, axis, [(i, (i + d) % size) for i in range(size)])]
    pallas_call x9 -> x8, Pallas kernels: 4.36 us -> 2.97 us  [small_call(): pl.pallas_call(lambda *refs: kernel(*refs[:count], *refs[len(given):outs]...]
    ppermute x4 -> x3, starting transfers between devices: 11.2 us -> 11.4 us  [shift_over(): return lax.ppermute(block, axis, [(i, i + 1) for i in range(size - 1)])]
    unnamed x28 -> x26, local copies, waits for them, and re-layouts: 3.25 us -> 3.26 us
  transfers between devices with their start and end apart: 25 -> 23, of which waited for: 8 -> 9; matrix products, arithmetic and copies ran while one was open for 0% -> 0% of each run, Pallas kernels for 14% -> 22%
where the time goes in v1:
time: 122 us; the launch traced here: 120 us
  starting transfers between devices  52.3 us (43%)
  waiting for transfers between devices  32.4 us (27%)
  Pallas kernels  31.4 us (26%)
  local copies, waits for them, and re-layouts  3.26 us (3%)
    ppermute x12, starting transfers between devices, rotate_over(): return lax.ppermute(block, axis, [(i, (i + d) % size) for i in range(size)])  33 us
    pallas_call x2, Pallas kernels, attention(): pl.pallas_call(kernel, grid=(count,), out_shape=[jax.ShapeDtypeStruct((ro...  23 us
    ppermute x12, waiting for transfers between devices, rotate_over(): return lax.ppermute(block, axis, [(i, (i + d) % size) for i in range(size)])  20.7 us
    ppermute x3, starting transfers between devices, shift_over(): return lax.ppermute(block, axis, [(i, i + 1) for i in range(size - 1)])  11.4 us
    ppermute x8, starting transfers between devices, swap_over(): return lax.ppermute(block, axis, [(0, 1), (1, 0)])  7.89 us
    ppermute x8, waiting for transfers between devices, swap_over(): return lax.ppermute(block, axis, [(0, 1), (1, 0)])  6.99 us
    ppermute x3, waiting for transfers between devices, shift_over(): return lax.ppermute(block, axis, [(i, i + 1) for i in range(size - 1)])  4.67 us
    pallas_call x1, Pallas kernels, down_project(): pl.pallas_call(functools.partial(down_kernel, tenants, rank), out_shape=j...  3.37 us
  transfers between devices with their start and end apart: 23, of which 9 were waited for; matrix products, arithmetic and copies ran while one was open for 0% of the time, Pallas kernels for 22%

profile of v1, /device:TPU:0, one launch (start us, length us, event | category | flops | bytes accessed | tf_op | source)
XLA Modules:
  0.0 120.3 jit_solution(7941945181558500714)
XLA Ops:
  0.6 1.9 %pack_keys_values.1.own.refs_3_.refs_4_.refs_11_ = bf16[272,1024]{1,0:T(8,128)(2,1)} custom-call(bf16[256,512]{1,0:T(8,128)(2,1)} %keys.1, bf16[256,512]{1,0:T(8,128)(2,1)} %values.1, s32[1,256]{1,0:T(1,128)} %bitcast.10), custom_call_target="tpu_custom_call" | custom-call | bytes 1048576 | tf_op jit(solution)/shard_map/pack_keys_values/pallas_call | solution.py:68
  2.5 0.0 copy-start.1
  2.5 5.1 %collective-permute-start = (bf16[272,1024]{1,0:T(8,128)(2,1)}, bf16[272,1024]{1,0:T(8,128)(2,1)S(1)}, u32[]{:S(2)}, u32[]{:S(2)}) collective-permute-start(bf16[272,1024]{1,0:T(8,128)(2,1)} %pack_keys_values.1.own.refs_3_.refs_4_.refs_11_), channel_id=1, source_target_pairs={{0,4},{4,8},{8,12},{1,5},{5,9},{9,13},{2,6},{6,10},{10,14},{3,7},{... | collective-permute-start | bytes 1671176 | tf_op jit(solution)/shard_map/ppermute | solution.py:536
  7.6 3.4 %down_project.1.refs_15_.refs_16_.refs_2_ = f32[24,256]{1,0:T(8,128)} custom-call(bf16[256,2560]{1,0:T(8,128)(2,1)} %refs_3_.1, bf16[128,2560]{1,0:T(8,128)(2,1)} %bitcast.9, s32[1,256]{1,0:T(1,128)} %bitcast.11, s32[16]{0:T(128)} %tenant_of.1), custom_call_target="tpu_custom_call" | custom-call | flops 167772160 | bytes 1966080 | tf_op jit(solution)/shard_map/down_project/pallas_call | solution.py:170
  11.0 1.6 %collective-permute-start.1 = (f32[24,256]{1,0:T(8,128)}, f32[24,256]{1,0:T(8,128)S(1)}, u32[]{:S(2)}, u32[]{:S(2)}) collective-permute-start(f32[24,256]{1,0:T(8,128)} %down_project.1.refs_15_.refs_16_.refs_2_), channel_id=1, source_target_pairs={{0,2},{2,0},{1,3},{3,1},{4,6},{6,4},{5,7},{7,5},{8,10},{10,8},{9,1... | collective-permute-start | bytes 73736 | tf_op jit(solution)/shard_map/ppermute | solution.py:520
  12.6 2.5 %collective-permute-done.1.after.refs_17_ = f32[24,256]{1,0:T(8,128)S(1)} collective-permute-done((f32[24,256]{1,0:T(8,128)}, f32[24,256]{1,0:T(8,128)S(1)}, u32[]{:S(2)}, u32[]{:S(2)}) %collective-permute-start.1) | collective-permute-done | bytes 24608 | tf_op jit(solution)/shard_map/ppermute | solution.py:520
  15.1 4.7 %collective-permute-done.got = bf16[272,1024]{1,0:T(8,128)(2,1)S(1)} collective-permute-done((bf16[272,1024]{1,0:T(8,128)(2,1)}, bf16[272,1024]{1,0:T(8,128)(2,1)S(1)}, u32[]{:S(2)}, u32[]{:S(2)}) %collective-permute-start) | collective-permute-done | bytes 557088 | tf_op jit(solution)/shard_map/ppermute | solution.py:536
  19.8 0.2 relay_block.1
  20.0 0.1 collective-permute-start.2
  20.1 2.4 %collective-permute-start.4 = (bf16[272,512]{1,0:T(8,128)(2,1)S(1)}, bf16[272,512]{1,0:T(8,128)(2,1)S(1)}, u32[]{:S(2)}, u32[]{:S(2)}) collective-permute-start(bf16[272,512]{1,0:T(8,128)(2,1)S(1)} %get-tuple-element.28), channel_id=1, source_target_pairs={{0,1},{1,4},{4,5},{5,8},{8,9},{9,12},{12,13},{2,3},{3,6},{6,7},{7,... | collective-permute-start | bytes 835592 | tf_op jit(solution)/shard_map/ppermute | solution.py:536
  22.5 3.9 %collective-permute-start.3 = (bf16[272,512]{1,0:T(8,128)(2,1)S(1)}, bf16[272,512]{1,0:T(8,128)(2,1)S(1)}, u32[]{:S(2)}, u32[]{:S(2)}) collective-permute-start(bf16[272,512]{1,0:T(8,128)(2,1)S(1)} %get-tuple-element.27), channel_id=1, source_target_pairs={{0,1},{1,4},{4,5},{5,8},{8,9},{9,12},{12,13},{2,3},{3,6},{6,7},{7,... | collective-permute-start | bytes 835592 | tf_op jit(solution)/shard_map/ppermute | solution.py:536
  26.5 0.7 copy-done.10
  27.2 0.2 copy-done.9
  27.4 11.4 %attention.2 = (bf16[256,4096]{1,0:T(8,128)(2,1)}, bf16[64,2048]{1,0:T(8,128)(2,1)}, bf16[64,2048]{1,0:T(8,128)(2,1)}, f32[16,256]{1,0:T(8,128)}) custom-call(bf16[256,4096]{1,0:T(8,128)(2,1)} %refs_0_.3, bf16[256,4096]{1,0:T(8,128)(2,1)} %refs_1_.3, bf16[128,4096]{1,0:T(8,128)(2,1)} %bitcast.14, ...), custom_call_target="tpu_custom_call" | custom-call | flops 4294967296 | bytes 3145728 | tf_op jit(solution)/shard_map/attention/pallas_call | solution.py:354
  38.8 4.0 %collective-permute-start.5 = (bf16[64,2048]{1,0:T(8,128)(2,1)}, bf16[64,2048]{1,0:T(8,128)(2,1)S(1)}, u32[]{:S(2)}, u32[]{:S(2)}) collective-permute-start(bf16[64,2048]{1,0:T(8,128)(2,1)} %get-tuple-element.33), channel_id=1, source_target_pairs={{0,1},{1,0},{2,3},{3,2},{4,5},{5,4},{6,7},{7,6},{8,9},{9,8},{10,11... | collective-permute-start | bytes 786440 | tf_op jit(solution)/shard_map/ppermute | solution.py:520
  42.8 0.7 copy-done.11
  43.5 11.6 %attention.3 = (bf16[256,4096]{1,0:T(8,128)(2,1)}, bf16[64,2048]{1,0:T(8,128)(2,1)}, bf16[64,2048]{1,0:T(8,128)(2,1)}, f32[16,256]{1,0:T(8,128)}) custom-call(bf16[256,4096]{1,0:T(8,128)(2,1)} %refs_0_.3, bf16[256,4096]{1,0:T(8,128)(2,1)} %refs_1_.3, bf16[128,4096]{1,0:T(8,128)(2,1)} %bitcast.15, ...), custom_call_target="tpu_custom_call", output_to_operand_aliasing={{0}: (19, {})} | custom-call | flops 4294967296 | bytes 3145728 | tf_op jit(solution)/shard_map/attention/pallas_call | solution.py:354
  55.1 0.9 copy-done.2
  56.1 0.1 scatter_grads.2
  56.2 5.7 %collective-permute-start.6 = (bf16[16,2048]{1,0:T(8,128)(2,1)S(1)}, bf16[16,2048]{1,0:T(8,128)(2,1)S(1)}, u32[]{:S(2)}, u32[]{:S(2)}) collective-permute-start(bf16[16,2048]{1,0:T(8,128)(2,1)S(1)} %get-tuple-element.36), channel_id=1, source_target_pairs={{0,4},{4,8},{8,12},{12,0},{1,5},{5,9},{9,13},{13,1},{2,6},{6,10},{... | collective-permute-start | bytes 196616 | tf_op jit(solution)/shard_map/ppermute | solution.py:525
  61.9 1.5 %collective-permute-start.13 = (f32[16,256]{1,0:T(8,128)}, f32[16,256]{1,0:T(8,128)S(1)}, u32[]{:S(2)}, u32[]{:S(2)}) collective-permute-start(f32[16,256]{1,0:T(8,128)} %get-tuple-element.40.refs_0_), channel_id=1, source_target_pairs={{0,2},{2,0},{1,3},{3,1},{4,6},{6,4},{5,7},{7,5},{8,10},{10,8},{9,1... | collective-permute-start | bytes 49160 | tf_op jit(solution)/shard_map/ppermute | solution.py:520
  63.4 2.4 %collective-permute-done.13.refs_1_ = f32[16,256]{1,0:T(8,128)S(1)} collective-permute-done((f32[16,256]{1,0:T(8,128)}, f32[16,256]{1,0:T(8,128)S(1)}, u32[]{:S(2)}, u32[]{:S(2)}) %collective-permute-start.13) | collective-permute-done | bytes 16416 | tf_op jit(solution)/shard_map/ppermute | solution.py:520
  65.9 0.7 copy-done.8
  66.6 0.4 split_grads.1
  67.0 0.3 collective-permute-start.14
  67.3 0.2 collective-permute-start.12
  67.6 7.2 %collective-permute-start.7 = (bf16[16,2048]{1,0:T(8,128)(2,1)S(1)}, bf16[16,2048]{1,0:T(8,128)(2,1)S(1)}, u32[]{:S(2)}, u32[]{:S(2)}) collective-permute-start(bf16[16,2048]{1,0:T(8,128)(2,1)S(1)} %get-tuple-element.37), channel_id=1, source_target_pairs={{0,8},{4,12},{8,0},{12,4},{1,9},{5,13},{9,1},{13,5},{2,10},{6,14},... | collective-permute-start | bytes 196616 | tf_op jit(solution)/shard_map/ppermute | solution.py:525
  74.8 2.6 %collective-permute-start.8 = (bf16[16,2048]{1,0:T(8,128)(2,1)S(1)}, bf16[16,2048]{1,0:T(8,128)(2,1)S(1)}, u32[]{:S(2)}, u32[]{:S(2)}) collective-permute-start(bf16[16,2048]{1,0:T(8,128)(2,1)S(1)} %get-tuple-element.38), channel_id=1, source_target_pairs={{0,12},{4,0},{8,4},{12,8},{1,13},{5,1},{9,5},{13,9},{2,14},{6,2},{... | collective-permute-start | bytes 196616 | tf_op jit(solution)/shard_map/ppermute | solution.py:525
  77.4 1.9 %collective-permute-done.8.refs_3_ = bf16[16,2048]{1,0:T(8,128)(2,1)S(1)} collective-permute-done((bf16[16,2048]{1,0:T(8,128)(2,1)S(1)}, bf16[16,2048]{1,0:T(8,128)(2,1)S(1)}, u32[]{:S(2)}, u32[]{:S(2)}) %collective-permute-start.8) | collective-permute-done | bytes 65568 | tf_op jit(solution)/shard_map/ppermute | solution.py:525
  79.3 0.3 scatter_grads.3
  79.7 1.5 %collective-permute-start.15 = (bf16[16,4608]{1,0:T(8,128)(2,1)S(1)}, bf16[16,4608]{1,0:T(8,128)(2,1)S(1)}, u32[]{:S(2)}, u32[]{:S(2)}) collective-permute-start(bf16[16,4608]{1,0:T(8,128)(2,1)S(1)} %get-tuple-element.44), channel_id=1, source_target_pairs={{0,4},{4,8},{8,12},{12,0},{1,5},{5,9},{9,13},{13,1},{2,6},{6,10},{... | collective-permute-start | bytes 442376 | tf_op jit(solution)/shard_map/ppermute | solution.py:525
  81.1 3.3 %collective-permute-start.16 = (bf16[16,4608]{1,0:T(8,128)(2,1)S(1)}, bf16[16,4608]{1,0:T(8,128)(2,1)S(1)}, u32[]{:S(2)}, u32[]{:S(2)}) collective-permute-start(bf16[16,4608]{1,0:T(8,128)(2,1)S(1)} %get-tuple-element.45), channel_id=1, source_target_pairs={{0,8},{4,12},{8,0},{12,4},{1,9},{5,13},{9,1},{13,5},{2,10},{6,14},... | collective-permute-start | bytes 442376 | tf_op jit(solution)/shard_map/ppermute | solution.py:525
  84.4 0.3 collective-permute-start.17
  84.8 1.1 collective-permute-start.11
  85.9 2.0 %collective-permute-start.10 = (bf16[16,2048]{1,0:T(8,128)(2,1)S(1)}, bf16[16,2048]{1,0:T(8,128)(2,1)S(1)}, u32[]{:S(2)}, u32[]{:S(2)}) collective-permute-start(bf16[16,2048]{1,0:T(8,128)(2,1)S(1)} %sum_grads.2.refs_4_.refs_0_), channel_id=1, source_target_pairs={{0,8},{4,12},{8,0},{12,4},{1,9},{5,13},{9,1},{13,5},{2,10},{6,14},... | collective-permute-start | bytes 196616 | tf_op jit(solution)/shard_map/ppermute | solution.py:525
  87.9 0.8 collective-permute-done.15.refs_1_
  88.8 6.9 %collective-permute-start.9 = (bf16[16,2048]{1,0:T(8,128)(2,1)S(1)}, bf16[16,2048]{1,0:T(8,128)(2,1)S(1)}, u32[]{:S(2)}, u32[]{:S(2)}) collective-permute-start(bf16[16,2048]{1,0:T(8,128)(2,1)S(1)} %sum_grads.2.refs_4_.refs_0_), channel_id=1, source_target_pairs={{0,4},{4,8},{8,12},{12,0},{1,5},{5,9},{9,13},{13,1},{2,6},{6,10},{... | collective-permute-start | bytes 196616 | tf_op jit(solution)/shard_map/ppermute | solution.py:525
  95.6 0.1 sum_grads.3.refs_4_.refs_0_
  95.7 5.9 %collective-permute-done.10.refs_2_ = bf16[16,2048]{1,0:T(8,128)(2,1)S(1)} collective-permute-done((bf16[16,2048]{1,0:T(8,128)(2,1)S(1)}, bf16[16,2048]{1,0:T(8,128)(2,1)S(1)}, u32[]{:S(2)}, u32[]{:S(2)}) %collective-permute-start.10) | collective-permute-done | bytes 65568 | tf_op jit(solution)/shard_map/ppermute | solution.py:525
  101.7 0.1 collective-permute-start.18
  101.8 1.0 collective-permute-start.21
  102.8 1.4 %collective-permute-start.19 = (bf16[16,4608]{1,0:T(8,128)(2,1)S(1)}, bf16[16,4608]{1,0:T(8,128)(2,1)S(1)}, u32[]{:S(2)}, u32[]{:S(2)}) collective-permute-start(bf16[16,4608]{1,0:T(8,128)(2,1)S(1)} %sum_grads.3.refs_4_.refs_0_), channel_id=1, source_target_pairs={{0,4},{4,8},{8,12},{12,0},{1,5},{5,9},{9,13},{13,1},{2,6},{6,10},{... | collective-permute-start | bytes 442376 | tf_op jit(solution)/shard_map/ppermute | solution.py:525
  104.1 5.0 %collective-permute-done.21.refs_3_ = bf16[16,4608]{1,0:T(8,128)(2,1)S(1)} collective-permute-done((bf16[16,4608]{1,0:T(8,128)(2,1)S(1)}, bf16[16,4608]{1,0:T(8,128)(2,1)S(1)}, u32[]{:S(2)}, u32[]{:S(2)}) %collective-permute-start.21) | collective-permute-done | bytes 147488 | tf_op jit(solution)/shard_map/ppermute | solution.py:525
  109.2 7.0 %collective-permute-done.20.refs_2_ = bf16[16,4608]{1,0:T(8,128)(2,1)S(1)} collective-permute-done((bf16[16,4608]{1,0:T(8,128)(2,1)S(1)}, bf16[16,4608]{1,0:T(8,128)(2,1)S(1)}, u32[]{:S(2)}, u32[]{:S(2)}) %collective-permute-start.20) | collective-permute-done | bytes 147488 | tf_op jit(solution)/shard_map/ppermute | solution.py:525
  116.2 0.1 gather_grads.3.refs_2_
  116.3 0.1 collective-permute-start.22
  116.3 2.0 %collective-permute-done.22.refs_3_ = bf16[64,4608]{1,0:T(8,128)(2,1)S(1)} collective-permute-done((bf16[64,4608]{1,0:T(8,128)(2,1)S(1)}, bf16[64,4608]{1,0:T(8,128)(2,1)S(1)}, u32[]{:S(2)}, u32[]{:S(2)}) %collective-permute-start.22) | collective-permute-done | bytes 589856 | tf_op jit(solution)/shard_map/ppermute | solution.py:520
  118.3 1.9 %finish_grads.1 = (f32[128,4096]{1,0:T(8,128)}, f32[128,2560]{1,0:T(8,128)}) custom-call(bf16[64,2048]{1,0:T(8,128)(2,1)S(1)} %gather_grads.2.refs_0_, bf16[64,2048]{1,0:T(8,128)(2,1)S(1)} %collective-permute-done.18.refs_4_.refs_1_, bf16[64,4608]{1,0:T(8,128)(2,1)S(1)} %gather_grads.3.refs_2_, bf16[64,4608]{1,0:T(8,128)(2,1)S(1)} %collective-permute-done.22.refs_3_), custom_call_target="tpu_custom_call" | custom-call | flops 1703936 | bytes 3407872 | tf_op jit(solution)/shard_map/finish_grads/pallas_call | solution.py:381
  (37 shorter events, 0.1 us)
Async XLA Ops:
  2.5 17.3 %copy-start.1 = (bf16[272,1024]{1,0:T(8,128)(2,1)S(1)}, bf16[272,1024]{1,0:T(8,128)(2,1)}, u32[]{:S(2)}) copy-start(bf16[272,1024]{1,0:T(8,128)(2,1)} %pack_keys_values.1.own.refs_3_.refs_4_.refs_11_) | copy-start | bytes 1671172
  2.5 17.2 %collective-permute-start = (bf16[272,1024]{1,0:T(8,128)(2,1)}, bf16[272,1024]{1,0:T(8,128)(2,1)S(1)}, u32[]{:S(2)}, u32[]{:S(2)}) collective-permute-start(bf16[272,1024]{1,0:T(8,128)(2,1)} %pack_keys_values.1.own.refs_3_.refs_4_.refs_11_), channel_id=1, source_target_pairs={{0,4},{4,8},{8,12},{1,5},{5,9},{9,13},{2,6},{6,10},{10,14},{3,7},{... | collective-permute-start | bytes 1671176 | tf_op jit(solution)/shard_map/ppermute | solution.py:536
  11.0 4.1 %collective-permute-start.1 = (f32[24,256]{1,0:T(8,128)}, f32[24,256]{1,0:T(8,128)S(1)}, u32[]{:S(2)}, u32[]{:S(2)}) collective-permute-start(f32[24,256]{1,0:T(8,128)} %down_project.1.refs_15_.refs_16_.refs_2_), channel_id=1, source_target_pairs={{0,2},{2,0},{1,3},{3,1},{4,6},{6,4},{5,7},{7,5},{8,10},{10,8},{9,1... | collective-permute-start | bytes 73736 | tf_op jit(solution)/shard_map/ppermute | solution.py:520
  15.1 11.4 %copy-start.7 = (f32[24,256]{1,0:T(8,128)}, f32[24,256]{1,0:T(8,128)S(1)}, u32[]{:S(2)}) copy-start(f32[24,256]{1,0:T(8,128)S(1)} %collective-permute-done.1.after.refs_17_) | copy-start | bytes 73732
  20.0 6.5 %copy-start.4 = (bf16[272,1024]{1,0:T(8,128)(2,1)}, bf16[272,1024]{1,0:T(8,128)(2,1)S(1)}, u32[]{:S(2)}) copy-start(bf16[272,1024]{1,0:T(8,128)(2,1)S(1)} %get-tuple-element.26.refs_5_.refs_6_.refs_12_) | copy-start | bytes 1671172
  20.0 6.4 %collective-permute-start.2 = (bf16[272,1024]{1,0:T(8,128)(2,1)S(1)}, bf16[272,1024]{1,0:T(8,128)(2,1)S(1)}, u32[]{:S(2)}, u32[]{:S(2)}) collective-permute-start(bf16[272,1024]{1,0:T(8,128)(2,1)S(1)} %get-tuple-element.26.refs_5_.refs_6_.refs_12_), channel_id=1, source_target_pairs={{0,1},{1,0},{2,3},{3,2},{4,5},{5,4},{6,7},{7,6},{8,9},{9,8},{10,11... | collective-permute-start | bytes 1671176 | tf_op jit(solution)/shard_map/ppermute | solution.py:520
  20.1 6.3 %collective-permute-start.4 = (bf16[272,512]{1,0:T(8,128)(2,1)S(1)}, bf16[272,512]{1,0:T(8,128)(2,1)S(1)}, u32[]{:S(2)}, u32[]{:S(2)}) collective-permute-start(bf16[272,512]{1,0:T(8,128)(2,1)S(1)} %get-tuple-element.28), channel_id=1, source_target_pairs={{0,1},{1,4},{4,5},{5,8},{8,9},{9,12},{12,13},{2,3},{3,6},{6,7},{7,... | collective-permute-start | bytes 835592 | tf_op jit(solution)/shard_map/ppermute | solution.py:536
  22.5 20.3 %collective-permute-start.3 = (bf16[272,512]{1,0:T(8,128)(2,1)S(1)}, bf16[272,512]{1,0:T(8,128)(2,1)S(1)}, u32[]{:S(2)}, u32[]{:S(2)}) collective-permute-start(bf16[272,512]{1,0:T(8,128)(2,1)S(1)} %get-tuple-element.27), channel_id=1, source_target_pairs={{0,1},{1,4},{4,5},{5,8},{8,9},{9,12},{12,13},{2,3},{3,6},{6,7},{7,... | collective-permute-start | bytes 835592 | tf_op jit(solution)/shard_map/ppermute | solution.py:536
  26.4 0.7 copy-start.10
  26.5 0.9 copy-start.9
  38.8 16.3 %collective-permute-start.5 = (bf16[64,2048]{1,0:T(8,128)(2,1)}, bf16[64,2048]{1,0:T(8,128)(2,1)S(1)}, u32[]{:S(2)}, u32[]{:S(2)}) collective-permute-start(bf16[64,2048]{1,0:T(8,128)(2,1)} %get-tuple-element.33), channel_id=1, source_target_pairs={{0,1},{1,0},{2,3},{3,2},{4,5},{5,4},{6,7},{7,6},{8,9},{9,8},{10,11... | collective-permute-start | bytes 786440 | tf_op jit(solution)/shard_map/ppermute | solution.py:520
  42.8 0.7 copy-start.11
  43.5 11.6 %copy-start.5 = (bf16[64,2048]{1,0:T(8,128)(2,1)S(1)}, bf16[64,2048]{1,0:T(8,128)(2,1)}, u32[]{:S(2)}) copy-start(bf16[64,2048]{1,0:T(8,128)(2,1)} %get-tuple-element.32.refs_0_) | copy-start | bytes 786436
  43.5 22.4 %copy-start = (bf16[256,2560]{1,0:T(8,128)(2,1)S(1)}, bf16[256,2560]{1,0:T(8,128)(2,1)}, u32[]{:S(2)}) copy-start(bf16[256,2560]{1,0:T(8,128)(2,1)} %refs_3_.1) | copy-start | bytes 3932164
  43.5 22.4 %copy-start.6 = (f32[24,256]{1,0:T(8,128)S(1)}, f32[24,256]{1,0:T(8,128)}, u32[]{:S(2)}) copy-start(f32[24,256]{1,0:T(8,128)} %down_project.1.refs_15_.refs_16_.refs_2_) | copy-start | bytes 73732
  55.1 1.0 copy-start.2
  56.1 11.3 %copy-start.12 = (bf16[64,2048]{1,0:T(8,128)(2,1)S(1)}, bf16[64,2048]{1,0:T(8,128)(2,1)}, u32[]{:S(2)}) copy-start(bf16[64,2048]{1,0:T(8,128)(2,1)} %get-tuple-element.39) | copy-start | bytes 786436
  56.1 23.3 %copy-start.3 = (bf16[64,2048]{1,0:T(8,128)(2,1)S(1)}, bf16[64,2048]{1,0:T(8,128)(2,1)}, u32[]{:S(2)}) copy-start(bf16[64,2048]{1,0:T(8,128)(2,1)} %get-tuple-element.34.refs_2_.refs_0_) | copy-start | bytes 786436
  56.2 9.7 %collective-permute-start.6 = (bf16[16,2048]{1,0:T(8,128)(2,1)S(1)}, bf16[16,2048]{1,0:T(8,128)(2,1)S(1)}, u32[]{:S(2)}, u32[]{:S(2)}) collective-permute-start(bf16[16,2048]{1,0:T(8,128)(2,1)S(1)} %get-tuple-element.36), channel_id=1, source_target_pairs={{0,4},{4,8},{8,12},{12,0},{1,5},{5,9},{9,13},{13,1},{2,6},{6,10},{... | collective-permute-start | bytes 196616 | tf_op jit(solution)/shard_map/ppermute | solution.py:525
  61.9 3.9 %collective-permute-start.13 = (f32[16,256]{1,0:T(8,128)}, f32[16,256]{1,0:T(8,128)S(1)}, u32[]{:S(2)}, u32[]{:S(2)}) collective-permute-start(f32[16,256]{1,0:T(8,128)} %get-tuple-element.40.refs_0_), channel_id=1, source_target_pairs={{0,2},{2,0},{1,3},{3,1},{4,6},{6,4},{5,7},{7,5},{8,10},{10,8},{9,1... | collective-permute-start | bytes 49160 | tf_op jit(solution)/shard_map/ppermute | solution.py:520
  65.9 0.7 copy-start.8
  67.0 12.3 %collective-permute-start.14 = (bf16[64,2560]{1,0:T(8,128)(2,1)S(1)}, bf16[64,2560]{1,0:T(8,128)(2,1)S(1)}, u32[]{:S(2)}, u32[]{:S(2)}) collective-permute-start(bf16[64,2560]{1,0:T(8,128)(2,1)S(1)} %get-tuple-element.42), channel_id=1, source_target_pairs={{0,1},{1,0},{2,3},{3,2},{4,5},{5,4},{6,7},{7,6},{8,9},{9,8},{10,11... | collective-permute-start | bytes 983048 | tf_op jit(solution)/shard_map/ppermute | solution.py:520
  67.3 12.0 %collective-permute-start.12 = (bf16[64,2048]{1,0:T(8,128)(2,1)S(1)}, bf16[64,2048]{1,0:T(8,128)(2,1)S(1)}, u32[]{:S(2)}, u32[]{:S(2)}) collective-permute-start(bf16[64,2048]{1,0:T(8,128)(2,1)S(1)} %copy-done.12), channel_id=1, source_target_pairs={{0,1},{1,0},{2,3},{3,2},{4,5},{5,4},{6,7},{7,6},{8,9},{9,8},{10,11... | collective-permute-start | bytes 786440 | tf_op jit(solution)/shard_map/ppermute | solution.py:520
  67.6 9.8 %collective-permute-start.7 = (bf16[16,2048]{1,0:T(8,128)(2,1)S(1)}, bf16[16,2048]{1,0:T(8,128)(2,1)S(1)}, u32[]{:S(2)}, u32[]{:S(2)}) collective-permute-start(bf16[16,2048]{1,0:T(8,128)(2,1)S(1)} %get-tuple-element.37), channel_id=1, source_target_pairs={{0,8},{4,12},{8,0},{12,4},{1,9},{5,13},{9,1},{13,5},{2,10},{6,14},... | collective-permute-start | bytes 196616 | tf_op jit(solution)/shard_map/ppermute | solution.py:525
  74.8 4.5 %collective-permute-start.8 = (bf16[16,2048]{1,0:T(8,128)(2,1)S(1)}, bf16[16,2048]{1,0:T(8,128)(2,1)S(1)}, u32[]{:S(2)}, u32[]{:S(2)}) collective-permute-start(bf16[16,2048]{1,0:T(8,128)(2,1)S(1)} %get-tuple-element.38), channel_id=1, source_target_pairs={{0,12},{4,0},{8,4},{12,8},{1,13},{5,1},{9,5},{13,9},{2,14},{6,2},{... | collective-permute-start | bytes 196616 | tf_op jit(solution)/shard_map/ppermute | solution.py:525
  79.7 9.1 %collective-permute-start.15 = (bf16[16,4608]{1,0:T(8,128)(2,1)S(1)}, bf16[16,4608]{1,0:T(8,128)(2,1)S(1)}, u32[]{:S(2)}, u32[]{:S(2)}) collective-permute-start(bf16[16,4608]{1,0:T(8,128)(2,1)S(1)} %get-tuple-element.44), channel_id=1, source_target_pairs={{0,4},{4,8},{8,12},{12,0},{1,5},{5,9},{9,13},{13,1},{2,6},{6,10},{... | collective-permute-start | bytes 442376 | tf_op jit(solution)/shard_map/ppermute | solution.py:525
  81.1 14.5 %collective-permute-start.16 = (bf16[16,4608]{1,0:T(8,128)(2,1)S(1)}, bf16[16,4608]{1,0:T(8,128)(2,1)S(1)}, u32[]{:S(2)}, u32[]{:S(2)}) collective-permute-start(bf16[16,4608]{1,0:T(8,128)(2,1)S(1)} %get-tuple-element.45), channel_id=1, source_target_pairs={{0,8},{4,12},{8,0},{12,4},{1,9},{5,13},{9,1},{13,5},{2,10},{6,14},... | collective-permute-start | bytes 442376 | tf_op jit(solution)/shard_map/ppermute | solution.py:525
  84.4 11.2 %collective-permute-start.17 = (bf16[16,4608]{1,0:T(8,128)(2,1)S(1)}, bf16[16,4608]{1,0:T(8,128)(2,1)S(1)}, u32[]{:S(2)}, u32[]{:S(2)}) collective-permute-start(bf16[16,4608]{1,0:T(8,128)(2,1)S(1)} %get-tuple-element.46), channel_id=1, source_target_pairs={{0,12},{4,0},{8,4},{12,8},{1,13},{5,1},{9,5},{13,9},{2,14},{6,2},{... | collective-permute-start | bytes 442376 | tf_op jit(solution)/shard_map/ppermute | solution.py:525
  84.8 11.0 %collective-permute-start.11 = (bf16[16,2048]{1,0:T(8,128)(2,1)S(1)}, bf16[16,2048]{1,0:T(8,128)(2,1)S(1)}, u32[]{:S(2)}, u32[]{:S(2)}) collective-permute-start(bf16[16,2048]{1,0:T(8,128)(2,1)S(1)} %sum_grads.2.refs_4_.refs_0_), channel_id=1, source_target_pairs={{0,12},{4,0},{8,4},{12,8},{1,13},{5,1},{9,5},{13,9},{2,14},{6,2},{... | collective-permute-start | bytes 196616 | tf_op jit(solution)/shard_map/ppermute | solution.py:525
  85.9 15.7 %collective-permute-start.10 = (bf16[16,2048]{1,0:T(8,128)(2,1)S(1)}, bf16[16,2048]{1,0:T(8,128)(2,1)S(1)}, u32[]{:S(2)}, u32[]{:S(2)}) collective-permute-start(bf16[16,2048]{1,0:T(8,128)(2,1)S(1)} %sum_grads.2.refs_4_.refs_0_), channel_id=1, source_target_pairs={{0,8},{4,12},{8,0},{12,4},{1,9},{5,13},{9,1},{13,5},{2,10},{6,14},... | collective-permute-start | bytes 196616 | tf_op jit(solution)/shard_map/ppermute | solution.py:525
  88.8 12.9 %collective-permute-start.9 = (bf16[16,2048]{1,0:T(8,128)(2,1)S(1)}, bf16[16,2048]{1,0:T(8,128)(2,1)S(1)}, u32[]{:S(2)}, u32[]{:S(2)}) collective-permute-start(bf16[16,2048]{1,0:T(8,128)(2,1)S(1)} %sum_grads.2.refs_4_.refs_0_), channel_id=1, source_target_pairs={{0,4},{4,8},{8,12},{12,0},{1,5},{5,9},{9,13},{13,1},{2,6},{6,10},{... | collective-permute-start | bytes 196616 | tf_op jit(solution)/shard_map/ppermute | solution.py:525
  101.7 14.5 %collective-permute-start.18 = (bf16[64,2048]{1,0:T(8,128)(2,1)S(1)}, bf16[64,2048]{1,0:T(8,128)(2,1)S(1)}, u32[]{:S(2)}, u32[]{:S(2)}) collective-permute-start(bf16[64,2048]{1,0:T(8,128)(2,1)S(1)} %gather_grads.2.refs_0_), channel_id=1, source_target_pairs={{0,1},{1,0},{2,3},{3,2},{4,5},{5,4},{6,7},{7,6},{8,9},{9,8},{10,11... | collective-permute-start | bytes 786440 | tf_op jit(solution)/shard_map/ppermute | solution.py:520
  101.8 7.4 %collective-permute-start.21 = (bf16[16,4608]{1,0:T(8,128)(2,1)S(1)}, bf16[16,4608]{1,0:T(8,128)(2,1)S(1)}, u32[]{:S(2)}, u32[]{:S(2)}) collective-permute-start(bf16[16,4608]{1,0:T(8,128)(2,1)S(1)} %sum_grads.3.refs_4_.refs_0_), channel_id=1, source_target_pairs={{0,12},{4,0},{8,4},{12,8},{1,13},{5,1},{9,5},{13,9},{2,14},{6,2},{... | collective-permute-start | bytes 442376 | tf_op jit(solution)/shard_map/ppermute | solution.py:525
  102.8 13.4 %collective-permute-start.20 = (bf16[16,4608]{1,0:T(8,128)(2,1)S(1)}, bf16[16,4608]{1,0:T(8,128)(2,1)S(1)}, u32[]{:S(2)}, u32[]{:S(2)}) collective-permute-start(bf16[16,4608]{1,0:T(8,128)(2,1)S(1)} %sum_grads.3.refs_4_.refs_0_), channel_id=1, source_target_pairs={{0,8},{4,12},{8,0},{12,4},{1,9},{5,13},{9,1},{13,5},{2,10},{6,14},... | collective-permute-start | bytes 442376 | tf_op jit(solution)/shard_map/ppermute | solution.py:525
  102.8 13.4 %collective-permute-start.19 = (bf16[16,4608]{1,0:T(8,128)(2,1)S(1)}, bf16[16,4608]{1,0:T(8,128)(2,1)S(1)}, u32[]{:S(2)}, u32[]{:S(2)}) collective-permute-start(bf16[16,4608]{1,0:T(8,128)(2,1)S(1)} %sum_grads.3.refs_4_.refs_0_), channel_id=1, source_target_pairs={{0,4},{4,8},{8,12},{12,0},{1,5},{5,9},{9,13},{13,1},{2,6},{6,10},{... | collective-permute-start | bytes 442376 | tf_op jit(solution)/shard_map/ppermute | solution.py:525
  116.3 2.1 %collective-permute-start.22 = (bf16[64,4608]{1,0:T(8,128)(2,1)S(1)}, bf16[64,4608]{1,0:T(8,128)(2,1)S(1)}, u32[]{:S(2)}, u32[]{:S(2)}) collective-permute-start(bf16[64,4608]{1,0:T(8,128)(2,1)S(1)} %gather_grads.3.refs_2_), channel_id=1, source_target_pairs={{0,1},{1,0},{2,3},{3,2},{4,5},{5,4},{6,7},{7,6},{8,9},{9,8},{10,11... | collective-permute-start | bytes 1769480 | tf_op jit(solution)/shard_map/ppermute | solution.py:520
